TPU v7x, 512 devices: a whole 4x8x8 slice. The times are simulated.
512 devices in a mesh: ctx: 64 (over z, x, core), head: 8 (over y).
Axes of the slice: x: 4, y: 8, z: 8, core: 2. Of those that a mesh axis runs over, the one named last changes fastest.
Arguments:
- video_q: bfloat16 [4096, 3072], P('ctx', 'head'), may hold values from -51 to 51
- video_k: bfloat16 [4096, 3072], P('ctx', 'head'), may hold values from -4 to 4
- video_v: bfloat16 [4096, 3072], P('ctx', 'head'), may hold values from -6 to 6
- text_q: bfloat16 [256, 3072], P(None, 'head'), may hold values from -51 to 51
- text_k: bfloat16 [256, 3072], P(None, 'head'), may hold values from -4 to 4
- text_v: bfloat16 [256, 3072], P(None, 'head'), may hold values from -6 to 6
- tile_mask: int32 [32, 32], replicated, may hold values from 0 to 1, as said below
- out_weight: bfloat16 [3072, 3072], P('head'), may hold values from -0.109375 to 0.109375
Outputs:
- video_out: bfloat16 [4096, 3072], P('ctx', 'head')
- text_out: bfloat16 [256, 3072], P(None, 'head')
Inputs may be any that keep to these rules, and one draw needn't show every extreme that they name: `tile_mask`: with tile t in frame t // 4 at position t % 4, entry [i, j] is 1 exactly when |position_i - position_j| * (1 + |frame_i - frame_j|) <= reach_i, for a reach_i of query tile i between 0 and 4; so every query tile reaches the tile at its own position in every frame.
All inputs are finite; a program needn't handle non-finite values.
Results may differ from a plain program's by a relative error of at most 0.029.
Values may be sent and summed in bfloat16 or wider, within the bound.
A program may use at most 192 MiB of HBM per device.

v0:
```python
import math

import jax
import jax.numpy as jnp
from jax import lax
from jax.sharding import PartitionSpec as P

HEAD_DIM = 128
TILE = 128


def split_heads(matrix):
    return matrix.reshape(matrix.shape[0], matrix.shape[1] // HEAD_DIM, HEAD_DIM)


def fresh_state(local_heads, query_count):
    return (
        jnp.full((local_heads, query_count), -1e30, jnp.float32),
        jnp.zeros((local_heads, query_count), jnp.float32),
        jnp.zeros((local_heads, query_count, HEAD_DIM), jnp.float32),
    )


def absorb(state, queries, key_rows, value_rows, allowed):
    highest, row_total, summed = state
    scores = jnp.einsum("qhd,khd->hqk", queries, key_rows, preferred_element_type=jnp.float32)
    scores = scores * (1.0 / math.sqrt(HEAD_DIM))
    if allowed is not None:
        scores = jnp.where(allowed[None], scores, -1e30)
    new_high = jnp.maximum(highest, jnp.max(scores, axis=2))
    unnormalized = jnp.exp(scores - new_high[:, :, None])
    factor = jnp.exp(highest - new_high)
    row_total = row_total * factor + jnp.sum(unnormalized, axis=2)
    summed = summed * factor[:, :, None] + jnp.einsum(
        "hqk,khd->hqd",
        unnormalized.astype(jnp.bfloat16),
        value_rows,
        preferred_element_type=jnp.float32,
    )
    return (new_high, row_total, summed)


def finish(state):
    highest, row_total, summed = state
    result = summed / row_total[:, :, None]
    result = jnp.transpose(result, (1, 0, 2))
    return result.reshape(result.shape[0], result.shape[1] * result.shape[2]).astype(jnp.bfloat16)


def local(video_q, video_k, video_v, text_q, text_k, text_v, tile_mask, out_weight):
    row_count = video_q.shape[0]
    local_heads = video_q.shape[1] // HEAD_DIM
    my_index = lax.axis_index("ctx")
    first_row = my_index * row_count
    query_tiles = (first_row + jnp.arange(row_count)) // TILE
    mask_rows = jnp.take(tile_mask, query_tiles, axis=0)
    video_q3 = split_heads(video_q)
    text_q3 = split_heads(text_q)
    text_k3 = split_heads(text_k)
    text_v3 = split_heads(text_v)
    video_init = absorb(fresh_state(local_heads, row_count), video_q3, text_k3, text_v3, None)
    text_init = absorb(fresh_state(local_heads, text_q3.shape[0]), text_q3, text_k3, text_v3, None)
    key_rows = split_heads(lax.all_gather(video_k, "ctx", axis=0, tiled=True))
    value_rows = split_heads(lax.all_gather(video_v, "ctx", axis=0, tiled=True))
    key_tiles = jnp.arange(key_rows.shape[0]) // TILE
    allowed = jnp.take(mask_rows, key_tiles, axis=1) > 0
    video_next = absorb(video_init, video_q3, key_rows, value_rows, allowed)
    text_next = absorb(text_init, text_q3, key_rows, value_rows, None)
    text_out = finish(text_next)
    video_attn = finish(video_next)
    video_out = (
        lax.psum_scatter(
            lax.dot_general(
                out_weight, video_attn, (((0,), (1,)), ((), ())), preferred_element_type=jnp.float32
            ).astype(jnp.bfloat16),
            "head",
            scatter_dimension=0,
            tiled=True,
        )
        .astype(jnp.float32)
        .T
    )
    return (video_out.astype(jnp.bfloat16), text_out)


def solution(mesh):
    placed = (
        P("ctx", "head"),
        P("ctx", "head"),
        P("ctx", "head"),
        P(None, "head"),
        P(None, "head"),
        P(None, "head"),
        P(),
        P("head", None),
    )
    return jax.shard_map(
        local,
        mesh=mesh,
        in_specs=placed,
        out_specs=(P("ctx", "head"), P(None, "head")),
        check_vma=False,
    )
```

profile of v0, /device:TPU:1, one launch (start us, length us, event | category | flops | bytes accessed | tf_op | source)
XLA Modules:
  0.0 237.3 jit_solution(3366570354070006961)
XLA Ops:
  7.2 0.0 copy-start
  7.2 0.0 all-gather.3.cloned.1.call-start
  7.2 0.7 all-gather.3.cloned.1.call-update
  7.9 0.0 all-gather.5.cloned.1.call-start
  8.0 0.7 all-gather.5.cloned.1.call-update
  8.7 0.0 reduce-scatter.4.cloned.1.call-start
  8.7 1.7 copy.46
  10.5 1.1 copy.43
  11.5 0.0 copy-start.4
  11.6 1.4 gather_fusion
  12.9 0.1 broadcast_select_fusion
  13.0 0.1 copy.48
  13.1 14.1 %gather_fusion.1 = s32[4096,64]{1,0:T(8,128)} fusion(s32[64,32]{0,1:T(8,128)S(1)} %copy.48, s32[4096]{0:T(1024)S(1)} %broadcast_clamp_fusion), kind=kCustom, calls=%fused_computation.1 | custom fusion | bytes 2113536 | tf_op jit(solution)/shard_map/jit(_take)/gather | solution.py:66
  27.2 3.6 %fusion.10 = pred[64,4096]{0,1:T(8,128)(4,1)S(1)} fusion(s32[4096,64]{1,0:T(8,128)} %gather_fusion.1, pred[4096]{0:T(1024)(128)(4,1)S(1)} %fusion.57), kind=kLoop, calls=%fused_computation.17 | loop fusion | flops 524288 | bytes 1314816 | tf_op jit(solution)/shard_map/gt | solution.py:66
  30.9 0.7 copy.49
  31.5 1.7 copy.56
  33.3 0.0 copy-done.4
  33.3 0.0 copy-done.8
  33.3 0.8 fusion.74
  34.1 1.3 fusion.75
  35.5 66.4 %all-gather.3.cloned.1.call-done = bf16[4096,384]{1,0:T(8,128)(2,1)} async-done(((bf16[64,384]{1,0:T(8,128)(2,1)}), bf16[4096,384]{1,0:T(8,128)(2,1)}) %all-gather.3.cloned.1.call-update) | async-done | bytes 3145744 | tf_op jit(solution)/shard_map/all_gather | solution.py:63
  101.8 4.8 %copy.50 = bf16[4096,384]{0,1:T(8,128)(2,1)} copy(bf16[4096,384]{1,0:T(8,128)(2,1)} %all-gather.3.cloned.1.call-done) | data formatting | bytes 6291456 | tf_op jit(solution)/shard_map/all_gather | solution.py:63
  106.6 3.0 %fusion.73 = (f32[3,64]{1,0:T(4,128)S(1)}, f32[3,64,4096]{2,1,0:T(8,128)S(1)}) fusion(bf16[4096,3,128]{0,2,1:T(8,128)(2,1)} %bitcast.119, pred[64,4096]{1,0:T(8,128)(4,1)S(1)} %copy.49, bf16[64,384]{1,0:T(8,128)(2,1)S(1)} %copy-done.8), kind=kOutput, calls=%fused_computation.103 | convolution fusion | flops 203685696 | bytes 6603520 | tf_op jit(solution)/shard_map/qhd,khd->hqk/dot_general | solution.py:26
  109.6 0.0 copy-start.2
  109.7 0.0 copy-start.3
  109.7 0.0 copy-done.5
  109.7 0.2 fusion.43
  109.9 1.4 copy-done.1
  111.3 0.6 fusion.8
  111.9 0.0 copy-done.6
  111.9 0.2 fusion.29
  112.1 0.5 copy-done.2
  112.7 0.0 copy-done.3
  112.7 6.5 %multiply_reduce_fusion = (f32[3,256]{1,0:T(4,128)S(1)}, f32[3,256,4096]{2,1,0:T(8,128)}) fusion(bf16[256,3,128]{0,2,1:T(8,128)(2,1)S(1)} %bitcast.124, bf16[4096,3,128]{0,2,1:T(8,128)(2,1)S(1)} %bitcast.120), kind=kOutput, calls=%fused_computation.3 | convolution fusion | flops 811597056 | bytes 15928320 | tf_op jit(solution)/shard_map/qhd,khd->hqk/dot_general | solution.py:26
  119.1 67.5 %all-gather.5.cloned.1.call-done = bf16[4096,384]{1,0:T(8,128)(2,1)} async-done(((bf16[64,384]{1,0:T(8,128)(2,1)}), bf16[4096,384]{1,0:T(8,128)(2,1)}) %all-gather.5.cloned.1.call-update) | async-done | bytes 3145744 | tf_op jit(solution)/shard_map/all_gather | solution.py:64
  186.6 4.7 %copy.53 = bf16[4096,384]{0,1:T(8,128)(2,1)} copy(bf16[4096,384]{1,0:T(8,128)(2,1)} %all-gather.5.cloned.1.call-done) | data formatting | bytes 6291456 | tf_op jit(solution)/shard_map/all_gather | solution.py:64
  191.3 4.1 %fusion.36 = bf16[3,8,8,128]{3,2,1,0:T(8,128)(2,1)S(1)} fusion(f32[64,3,128]{2,0,1:T(8,128)S(1)} %fusion.29, bf16[4096,3,128]{0,2,1:T(8,128)(2,1)} %bitcast.121, f32[3,64,4096]{2,1,0:T(8,128)} %copy-done.1, f32[3,64]{1,0:T(4,128)S(1)} %get-tuple-element.16, f32[64,3]{0,1:T(4,128)S(1)} %get-tuple-element.10), kind=kOutput, calls=%fused_computation.36 | convolution fusion | flops 202973184 | bytes 6440448 | tf_op jit(solution)/shard_map/hqk,khd->hqd/dot_general | solution.py:34
  195.4 0.5 fusion.7
  195.9 1.2 copy.72
  197.1 0.0 reduce-scatter.4.cloned.1.call-update
  197.2 7.0 %fusion.14 = f32[256,3,128]{0,2,1:T(8,128)S(1)} fusion(bf16[4096,3,128]{0,2,1:T(8,128)(2,1)} %bitcast.122, f32[3,256,4096]{2,1,0:T(8,128)} %get-tuple-element.25, f32[3,256]{1,0:T(4,128)S(1)} %get-tuple-element.14), kind=kOutput, calls=%fused_computation.21 | convolution fusion | flops 814743552 | bytes 16124928 | tf_op jit(solution)/shard_map/hqk,khd->hqd/dot_general | solution.py:34
  204.2 0.0 copy-start.7
  204.2 6.9 %fusion = f32[3,256]{1,0:T(4,128)S(1)} fusion(f32[3,256,4096]{2,1,0:T(8,128)} %get-tuple-element.25, f32[3,256]{1,0:T(4,128)S(1)} %get-tuple-element.14), kind=kLoop, calls=%fused_computation.4 | loop fusion | flops 9436416 | bytes 12589056 | tf_op jit(solution)/shard_map/reduce_sum | solution.py:33
  211.1 0.1 fusion.39
  211.2 0.3 fusion.21
  211.5 0.8 copy.62
  212.3 16.9 %reduce-scatter.4.cloned.1.call-done = bf16[384,64]{1,0:T(8,128)(2,1)} async-done(((bf16[3072,64]{1,0:T(8,128)(2,1)}), bf16[384,64]{1,0:T(8,128)(2,1)}) %reduce-scatter.4.cloned.1.call-update) | async-done | bytes 49168
  229.2 1.6 copy.73
  (16 shorter events, 0.1 us)
Async XLA Ops:
  7.2 188.2 %copy-start = (bf16[384,3072]{1,0:T(8,128)(2,1)S(1)}, bf16[384,3072]{1,0:T(8,128)(2,1)}, u32[]{:S(2)}) copy-start(bf16[384,3072]{1,0:T(8,128)(2,1)} %param.15) | copy-start | bytes 7077892
  7.2 94.7 %all-gather.3.cloned.1.call-start = ((), (), s32[]{:S(2)}) async-start(), calls=%async_computation.1 | async-start | bytes 3194880 | tf_op jit(solution)/shard_map/all_gather | solution.py:63
  7.9 178.7 %all-gather.5.cloned.1.call-start = ((), (), s32[]{:S(2)}) async-start(), calls=%async_computation.2 | async-start | bytes 3194880 | tf_op jit(solution)/shard_map/all_gather | solution.py:64
  8.7 220.5 %reduce-scatter.4.cloned.1.call-start = ((), (), s32[]{:S(2)}) async-start(), calls=%async_computation.3 | async-start | bytes 884736
  11.5 21.8 %copy-start.4 = (bf16[256,384]{0,1:T(8,128)(2,1)}, bf16[256,384]{0,1:T(8,128)(2,1)S(1)}, u32[]{:S(2)}) copy-start(bf16[256,384]{0,1:T(8,128)(2,1)S(1)} %copy.43) | copy-start | bytes 589828
  27.2 6.1 %copy-start.8 = (bf16[64,384]{1,0:T(8,128)(2,1)S(1)}, bf16[64,384]{1,0:T(8,128)(2,1)}, u32[]{:S(2)}) copy-start(bf16[64,384]{1,0:T(8,128)(2,1)} %param.8) | copy-start | bytes 147460
  106.6 3.1 %copy-start.5 = (f32[3,64,256]{2,1,0:T(8,128)S(1)}, f32[3,64,256]{2,1,0:T(8,128)}, u32[]{:S(2)}) copy-start(f32[3,64,256]{2,1,0:T(8,128)} %get-tuple-element.21) | copy-start | bytes 589828
  106.6 5.3 %copy-start.6 = (bf16[256,384]{0,1:T(8,128)(2,1)S(1)}, bf16[256,384]{0,1:T(8,128)(2,1)}, u32[]{:S(2)}) copy-start(bf16[256,384]{0,1:T(8,128)(2,1)} %copy.46) | copy-start | bytes 589828
  109.6 1.7 copy-start.1
  109.6 3.0 %copy-start.2 = (bf16[4096,384]{0,1:T(8,128)(2,1)S(1)}, bf16[4096,384]{0,1:T(8,128)(2,1)}, u32[]{:S(2)}) copy-start(bf16[4096,384]{0,1:T(8,128)(2,1)} %copy.50) | copy-start | bytes 9437188
  109.7 3.0 %copy-start.3 = (bf16[256,384]{0,1:T(8,128)(2,1)S(1)}, bf16[256,384]{0,1:T(8,128)(2,1)}, u32[]{:S(2)}) copy-start(bf16[256,384]{0,1:T(8,128)(2,1)} %copy.56) | copy-start | bytes 589828
  204.2 7.0 %copy-start.7 = (bf16[256,384]{0,1:T(8,128)(2,1)S(1)}, bf16[256,384]{0,1:T(8,128)(2,1)}, u32[]{:S(2)}) copy-start(bf16[256,384]{0,1:T(8,128)(2,1)} %copy.46) | copy-start | bytes 589828
Sparse Core Ops, SparseCore 0:
  11.4 90.4 all-gather.2
  105.2 81.3 all-gather.4
  197.3 31.8 reduce-scatter.3
where the time goes:
time: 242 us; the launch traced here: 237 us
  waiting for transfers between devices  152 us (63%)
  local copies, waits for them, and re-layouts  35.8 us (15%)
  matrix products  23.8 us (10%)
  between operations  13.9 us (6%)
  other arithmetic  11.6 us (5%)
    all_gather x1, waiting for transfers between devices, local(): value_rows = split_heads(lax.all_gather(video_v, 'ctx', axis=0, tiled=True))  67.5 us
    all_gather x1, waiting for transfers between devices, local(): key_rows = split_heads(lax.all_gather(video_k, 'ctx', axis=0, tiled=True))  66.4 us
    unnamed x4, waiting for transfers between devices  18.3 us
    gather x1, local copies, waits for them, and re-layouts, local(): allowed = jnp.take(mask_rows, key_tiles, axis=1) > 0  14.1 us
    dot_general x4, matrix products, absorb(): jnp.einsum('qhd,khd->hqk', queries, key_rows, preferred_element_type=jnp....  11.7 us
    dot_general x4, matrix products, absorb(): jnp.einsum('hqk,khd->hqd', unnormalized.astype(jnp.bfloat16), value_rows,...  11.6 us
    unnamed x24, local copies, waits for them, and re-layouts  10.2 us
    reduce_sum x4, other arithmetic, absorb(): row_total = row_total * factor + jnp.sum(unnormalized, axis=2)  7.75 us
  transfers between devices with their start and end apart: 3, of which 3 were waited for; matrix products, arithmetic and copies ran while one was open for 24% of the time, Pallas kernels for 0%

commit v1 on v0

v1 whole, which is shorter than its diff:
```python
import functools
import math

import jax
import jax.numpy as jnp
from jax import lax
from jax.experimental import pallas as pl
from jax.experimental.pallas import tpu as pltpu
from jax.sharding import PartitionSpec as P

HEAD_DIM = 128
ROWS = 64
HEADS = 3
NZ, NX, NY = 8, 4, 8
FEATURES = HEADS * HEAD_DIM
TXT_ROWS = 16
TXT_KEYS = 64
VIDEO_Q = NX * ROWS
QUERIES = VIDEO_Q + TXT_ROWS
MERGE = ROWS + TXT_ROWS
PACK = MERGE + 16
STEP_KEYS = 256
NEG = -1e30
SCALE = math.log2(math.e) / math.sqrt(HEAD_DIM)
MESH = pl.DeviceIdType.MESH
BF16, F32 = jnp.bfloat16, jnp.float32


def body(vq, vk, vv, tq, tk, tv, mask, w, out, tout,
         q, kv, tkv, bias, acc, top, osend, orecv, attn, wbuf, ysend, yrecv,
         load_sem, w_sem, q_send, q_recv, z_send, z_recv, s_send, s_recv,
         o_send, o_recv, y_send, y_recv, t_send, t_recv):
    ctx, y = lax.axis_index("ctx"), lax.axis_index("head")
    core, x, z = ctx % 2, (ctx // 2) % NX, ctx // (2 * NX)
    row_id = 2 * z + core

    def device(zz, xx, cc, yy):
        return ((zz * NX + xx) * 2 + cc, yy)

    def text_device(k):
        other = (row_id + k) % (2 * NZ)
        return device(other // 2, x, other % 2, y)

    up = device((z + 1) % NZ, x, core, y)
    down = device((z + NZ - 1) % NZ, x, core, y)
    sibling = device(z, x, 1 - core, y)

    def x_device(k):
        return device(z, (x + k) % NX, core, y)

    def y_device(k):
        return (ctx, (y + k) % NY)

    loads = []

    def load(src, dst):
        copy = pltpu.make_async_copy(src, dst, load_sem.at[len(loads)])
        copy.start()
        loads.append(copy)

    for h in range(HEADS):
        cols = pl.ds(h * HEAD_DIM, HEAD_DIM)
        load(vk.at[:, cols], kv.at[h, 0, core, 0])
        load(vv.at[:, cols], kv.at[h, 0, core, 1])
    load(vq, q.at[pl.ds(x * ROWS, ROWS)])
    load(tq.at[pl.ds(row_id * TXT_ROWS, TXT_ROWS)], q.at[pl.ds(VIDEO_Q, TXT_ROWS)])
    load(tk.at[pl.ds(x * TXT_KEYS, TXT_KEYS)], tkv.at[0, pl.ds(0, TXT_KEYS)])
    load(tv.at[pl.ds(x * TXT_KEYS, TXT_KEYS)], tkv.at[1, pl.ds(0, TXT_KEYS)])
    w_loads = []
    for k in range(NY):
        copy = pltpu.make_async_copy(
            w.at[:, pl.ds(((y + k) % NY) * FEATURES, FEATURES)], wbuf.at[k], w_sem.at[k])
        copy.start()
        w_loads.append(copy)

    barrier = pltpu.get_barrier_semaphore()
    peers = [text_device(k) for k in range(1, 2 * NZ)]
    peers += [x_device(k) for k in range(1, NX)]
    peers += [y_device(k) for k in range(1, NY)]
    for peer in peers:
        pl.semaphore_signal(barrier, inc=1, device_id=peer, device_id_type=MESH)

    zeros = jnp.zeros((QUERIES, HEAD_DIM), F32)
    for s in range(5):
        for half in range(2):
            cols = slice(half * HEAD_DIM, (half + 1) * HEAD_DIM)
            if s in (0, 4) and half == 1:
                if s == 0:
                    lane = lax.broadcasted_iota(jnp.int32, (QUERIES, HEAD_DIM), 1)
                    bias[0, :, cols] = jnp.where(lane < TXT_KEYS, 0.0, NEG).astype(F32)
                continue
            tile_z = (z + NZ - s) % NZ if half == 0 else (z + s) % NZ
            for xx in range(NX):
                reach = mask[z * NX + xx, tile_z * NX + x].astype(F32)
                bias[s, xx * ROWS:(xx + 1) * ROWS, cols] = jnp.full(
                    (ROWS, HEAD_DIM), (1.0 - reach) * NEG, F32)
            bias[s, VIDEO_Q:, cols] = zeros[:TXT_ROWS]
    tkv[0, TXT_KEYS:] = jnp.zeros((HEAD_DIM - TXT_KEYS, FEATURES), BF16)
    tkv[1, TXT_KEYS:] = jnp.zeros((HEAD_DIM - TXT_KEYS, FEATURES), BF16)

    for copy in loads:
        copy.wait()
    pl.semaphore_wait(barrier, len(peers))

    sent = []

    def remote(src, dst, send, recv, to):
        return pltpu.make_async_remote_copy(
            src_ref=src, dst_ref=dst, send_sem=send, recv_sem=recv,
            device_id=to, device_id_type=MESH)

    def start(copy):
        copy.start()
        sent.append(copy)

    def z_copy(h, direction, d):
        here = d - 1 if direction == 0 else (NZ - d + 1) % NZ
        there = d if direction == 0 else NZ - d
        src, dst = kv.at[h, here, core], kv.at[h, there, core]
        if d == 4:
            src, dst = src.at[direction], dst.at[direction]
        return remote(src, dst, z_send.at[h, direction, d - 1], z_recv.at[h, direction, d - 1],
                      up if direction == 0 else down)

    def s_copy(h, slot, part=None, cc=None):
        cc = core if cc is None else cc
        ref = kv.at[h, slot, cc]
        index = slot
        if part is not None:
            ref, index = ref.at[part], slot if part == 0 else NZ
        return remote(ref, ref, s_send.at[h, index], s_recv.at[h, index], sibling)

    for h in range(HEADS):
        for direction in range(2):
            start(z_copy(h, direction, 1))
        start(s_copy(h, 0))

    q_ref = q.at[pl.ds(x * ROWS, ROWS)]
    for k in range(1, NX):
        start(remote(q_ref, q_ref, q_send.at[k], q_recv.at[k], x_device(k)))

    def wait_q():
        for k in range(1, NX):
            ref = q.at[pl.ds(((x + NX - k) % NX) * ROWS, ROWS)]
            remote(ref, ref, q_send.at[k], q_recv.at[k], x_device(k)).wait_recv()

    ones = jnp.ones((STEP_KEYS, HEAD_DIM), BF16)

    def absorb(h, s):
        cols = slice(h * HEAD_DIM, (h + 1) * HEAD_DIM)
        slots = {0: (0,), 4: (4,)}.get(s, (s, NZ - s))
        keys = [kv[h, slot, cc, 0] for slot in slots for cc in range(2)]
        values = [kv[h, slot, cc, 1] for slot in slots for cc in range(2)]
        if s == 0:
            keys.append(tkv[0, :, cols])
            values.append(tkv[1, :, cols])
        keys, values = jnp.concatenate(keys, 0), jnp.concatenate(values, 0)
        count = keys.shape[0]
        scores = lax.dot_general(q[:, cols], keys, (((1,), (1,)), ((), ())),
                                 preferred_element_type=F32)
        scores = scores * SCALE + bias[s, :, :count]
        high = jnp.max(scores, axis=1, keepdims=True)
        if s:
            before = top[h][:, :1]
            high = jnp.maximum(high, before)
        weights = jnp.exp2(scores - high).astype(BF16)
        values = jnp.concatenate([values, ones[:count]], 1)
        summed = jnp.dot(weights, values, preferred_element_type=F32)
        if s:
            summed = summed + acc[h] * jnp.exp2(before - high)
        acc[h] = summed
        top[h] = jnp.broadcast_to(high, (QUERIES, HEAD_DIM))

    def forward(h, d):
        for direction in range(2):
            z_copy(h, direction, d).wait_recv()
            if d < 4:
                start(z_copy(h, direction, d + 1))
                start(s_copy(h, d if direction == 0 else NZ - d))
            else:
                start(s_copy(h, 4, direction))

    def from_sibling(h, s):
        if s == 4:
            s_copy(h, 4, 0, 1 - core).wait_recv()
            s_copy(h, 4, 1, 1 - core).wait_recv()
        else:
            for slot in ((0,) if s == 0 else (s, NZ - s)):
                s_copy(h, slot, None, 1 - core).wait_recv()

    for h in range(HEADS):
        from_sibling(h, 0)
    wait_q()
    for d in range(1, 5):
        for h in range(HEADS):
            forward(h, d)
            if d > 1:
                from_sibling(h, d - 1)
            absorb(h, d - 1)

    eye = (lax.broadcasted_iota(jnp.int32, (MERGE, HEAD_DIM), 0)
           == lax.broadcasted_iota(jnp.int32, (MERGE, HEAD_DIM), 1))
    pad = jnp.zeros((13, HEAD_DIM), F32)

    def o_copy(h, k):
        return remote(osend.at[h, k], orecv.at[h, k], o_send.at[h, k], o_recv.at[h, k], x_device(k))

    for h in range(HEADS):
        from_sibling(h, 4)
        absorb(h, 4)
        total = acc[h, :, HEAD_DIM:]
        part = acc[h, :, :HEAD_DIM] / total
        acc[h, :, :HEAD_DIM] = part
        acc[h, :, HEAD_DIM:] = top[h] + jnp.log2(total)
        for k in (2, 1, 3, 0):
            to = pl.ds(pl.multiple_of(((x + k) % NX) * ROWS, ROWS), ROWS)
            block = jnp.concatenate([acc[h, to, :HEAD_DIM], acc[h, VIDEO_Q:, :HEAD_DIM]], 0)
            level = jnp.concatenate([acc[h, to, HEAD_DIM:], acc[h, VIDEO_Q:, HEAD_DIM:]], 0)
            row = jnp.sum(jnp.where(eye, level, 0.0), axis=0, keepdims=True)
            first = row.astype(BF16).astype(F32)
            second = (row - first).astype(BF16).astype(F32)
            third = row - first - second
            stats = jnp.concatenate([first, second, third, pad], 0)
            packed = jnp.concatenate([block, stats], 0).astype(BF16)
            if k == 0:
                orecv[h, 0] = packed
            else:
                osend[h, k] = packed
                start(o_copy(h, k))

    for h in range(HEADS):
        for k in range(1, NX):
            o_copy(h, k).wait_recv()
        levels = []
        for k in range(NX):
            stats = orecv[h, k, MERGE:].astype(F32)
            row = stats[0:1] + stats[1:2] + stats[2:3]
            levels.append(jnp.sum(jnp.where(eye, jnp.broadcast_to(row, eye.shape), 0.0),
                                  axis=1, keepdims=True))
        high = functools.reduce(jnp.maximum, levels)
        shares = [jnp.exp2(level - high) for level in levels]
        total = functools.reduce(jnp.add, shares)
        merged = functools.reduce(
            jnp.add, [orecv[h, k, :MERGE].astype(F32) * (shares[k] / total) for k in range(NX)])
        attn[:, h * HEAD_DIM:(h + 1) * HEAD_DIM] = merged.astype(BF16)

    mine = pl.ds(pl.multiple_of(row_id * TXT_ROWS, TXT_ROWS), TXT_ROWS)
    tout[mine] = attn[ROWS:]

    def y_copy(k):
        return remote(ysend.at[k], yrecv.at[k], y_send.at[k], y_recv.at[k], y_device(k))

    for copy in w_loads:
        copy.wait()
    for k in (4, 3, 5, 2, 6, 1, 7):
        ysend[k] = jnp.dot(attn[:ROWS], wbuf[k], preferred_element_type=F32).astype(BF16)
        start(y_copy(k))
    for k in range(1, 2 * NZ):
        start(remote(tout.at[mine], tout.at[mine], t_send.at[k], t_recv.at[k], text_device(k)))
    total = jnp.dot(attn[:ROWS], wbuf[0], preferred_element_type=F32)
    for k in (1, 7, 2, 6, 3, 5, 4):
        y_copy(k).wait_recv()
        total = total + yrecv[k].astype(F32)
    out[...] = total.astype(BF16)

    for k in range(1, 2 * NZ):
        other = (row_id + 2 * NZ - k) % (2 * NZ)
        ref = tout.at[pl.ds(pl.multiple_of(other * TXT_ROWS, TXT_ROWS), TXT_ROWS)]
        remote(ref, ref, t_send.at[k], t_recv.at[k], text_device(k)).wait_recv()
    for copy in sent:
        copy.wait_send()


def local(video_q, video_k, video_v, text_q, text_k, text_v, tile_mask, out_weight):
    anywhere = pl.BlockSpec(memory_space=pl.ANY)
    vmem = pl.BlockSpec(memory_space=pltpu.VMEM)
    dma = pltpu.SemaphoreType.DMA
    return pl.pallas_call(
        body,
        out_shape=(
            jax.ShapeDtypeStruct((ROWS, FEATURES), BF16),
            jax.ShapeDtypeStruct((2 * NZ * TXT_ROWS, FEATURES), BF16),
        ),
        in_specs=[anywhere] * 6 + [pl.BlockSpec(memory_space=pltpu.SMEM), anywhere],
        out_specs=(vmem, vmem),
        scratch_shapes=[
            pltpu.VMEM((QUERIES, FEATURES), BF16),
            pltpu.VMEM((HEADS, NZ, 2, 2, ROWS, HEAD_DIM), BF16),
            pltpu.VMEM((2, HEAD_DIM, FEATURES), BF16),
            pltpu.VMEM((5, QUERIES, STEP_KEYS), F32),
            pltpu.VMEM((HEADS, QUERIES, 2 * HEAD_DIM), F32),
            pltpu.VMEM((HEADS, QUERIES, HEAD_DIM), F32),
            pltpu.VMEM((HEADS, NX, PACK, HEAD_DIM), BF16),
            pltpu.VMEM((HEADS, NX, PACK, HEAD_DIM), BF16),
            pltpu.VMEM((MERGE, FEATURES), BF16),
            pltpu.VMEM((NY, FEATURES, FEATURES), BF16),
            pltpu.VMEM((NY, ROWS, FEATURES), BF16),
            pltpu.VMEM((NY, ROWS, FEATURES), BF16),
            dma((10,)),
            dma((NY,)),
            dma((NX,)), dma((NX,)),
            dma((HEADS, 2, 4)), dma((HEADS, 2, 4)),
            dma((HEADS, NZ + 1)), dma((HEADS, NZ + 1)),
            dma((HEADS, NX)), dma((HEADS, NX)),
            dma((NY,)), dma((NY,)),
            dma((2 * NZ,)), dma((2 * NZ,)),
        ],
        compiler_params=pltpu.CompilerParams(
            collective_id=0, has_side_effects=True, vmem_limit_bytes=40 * 2**20),
    )(video_q, video_k, video_v, text_q, text_k, text_v, tile_mask, out_weight)


def solution(mesh):
    placed = (
        P("ctx", "head"),
        P("ctx", "head"),
        P("ctx", "head"),
        P(None, "head"),
        P(None, "head"),
        P(None, "head"),
        P(),
        P("head", None),
    )
    return jax.shard_map(
        local,
        mesh=mesh,
        in_specs=placed,
        out_specs=(P("ctx", "head"), P(None, "head")),
        check_vma=False,
    )
```

time: 242 us -> 61.1 us (0.25); the launches traced: 237 us -> 60.7 us
  waiting for transfers between devices: 152 us -> 0 us
  Pallas kernels: 0 us -> 51.2 us
  local copies, waits for them, and re-layouts: 35.8 us -> 8.85 us
  matrix products: 23.8 us -> 0 us
  between operations: 13.9 us -> 0.66 us
  other arithmetic: 11.6 us -> 0 us
    all_gather x2 -> x0, waiting for transfers between devices: 134 us -> none  [the longest x1 67.5 us: local(): value_rows = split_heads(lax.all_gather(video_v, 'ctx', axis=0, tiled=True))]
    pallas_call x0 -> x1, Pallas kernels: none -> 51.2 us  [local(): pl.pallas_call(body, out_shape=(jax.ShapeDtypeStruct((ROWS, FEATURES), BF...]
    dot_general x9 -> x0, matrix products: 23.8 us -> none  [the longest x4 11.7 us: absorb(): jnp.einsum('qhd,khd->hqk', queries, key_rows, preferred_element_type=jnp....]
    unnamed x4 -> x0, waiting for transfers between devices: 18.3 us -> none
    gather x2 -> x0, local copies, waits for them, and re-layouts: 15.4 us -> none  [the longest x1 14.1 us: local(): allowed = jnp.take(mask_rows, key_tiles, axis=1) > 0]
    all_gather x2 -> x0, local copies, waits for them, and re-layouts: 9.46 us -> none  [the longest x1 4.76 us: local(): key_rows = split_heads(lax.all_gather(video_k, 'ctx', axis=0, tiled=True))]
    reduce_sum x4 -> x0, other arithmetic: 7.75 us -> none  [absorb(): row_total = row_total * factor + jnp.sum(unnormalized, axis=2)]
    gt x1 -> x0, other arithmetic: 3.64 us -> none  [local(): allowed = jnp.take(mask_rows, key_tiles, axis=1) > 0]
  transfers between devices with their start and end apart: 3 -> 0, of which waited for: 3 -> 0; matrix products, arithmetic and copies ran while one was open for 24% -> 0% of each run, Pallas kernels for 0% -> 0%
where the time goes in v1:
time: 61.1 us; the launch traced here: 60.7 us
  Pallas kernels  51.2 us (84%)
  local copies, waits for them, and re-layouts  8.85 us (14%)
  between operations  0.66 us (1%)
    pallas_call x1, Pallas kernels, local(): pl.pallas_call(body, out_shape=(jax.ShapeDtypeStruct((ROWS, FEATURES), BF...  51.2 us
    unnamed x18, local copies, waits for them, and re-layouts  8.85 us

profile of v1, /device:TPU:1, one launch (start us, length us, event | category | flops | bytes accessed | tf_op | source)
XLA Modules:
  0.0 60.7 jit_solution(85955245786289593)
XLA Ops:
  0.6 0.0 copy-start
  0.6 1.7 %copy-done = bf16[384,3072]{1,0:T(8,128)(2,1)S(1)} copy-done((bf16[384,3072]{1,0:T(8,128)(2,1)S(1)}, bf16[384,3072]{1,0:T(8,128)(2,1)}, u32[]{:S(2)}) %copy-start) | copy-done | bytes 2359320
  2.3 0.0 copy-start.1
  2.3 0.9 %copy-done.1 = bf16[256,384]{1,0:T(8,128)(2,1)S(1)} copy-done((bf16[256,384]{1,0:T(8,128)(2,1)S(1)}, bf16[256,384]{1,0:T(8,128)(2,1)}, u32[]{:S(2)}) %copy-start.1) | copy-done | bytes 196632
  3.2 0.0 copy-start.2
  3.2 0.9 %copy-done.2 = bf16[256,384]{1,0:T(8,128)(2,1)S(1)} copy-done((bf16[256,384]{1,0:T(8,128)(2,1)S(1)}, bf16[256,384]{1,0:T(8,128)(2,1)}, u32[]{:S(2)}) %copy-start.2) | copy-done | bytes 196632
  4.2 0.0 copy-start.3
  4.2 0.9 %copy-done.3 = bf16[256,384]{1,0:T(8,128)(2,1)S(1)} copy-done((bf16[256,384]{1,0:T(8,128)(2,1)S(1)}, bf16[256,384]{1,0:T(8,128)(2,1)}, u32[]{:S(2)}) %copy-start.3) | copy-done | bytes 196632
  5.1 0.0 copy-start.4
  5.1 0.8 %copy-done.4 = bf16[64,384]{1,0:T(8,128)(2,1)S(1)} copy-done((bf16[64,384]{1,0:T(8,128)(2,1)S(1)}, bf16[64,384]{1,0:T(8,128)(2,1)}, u32[]{:S(2)}) %copy-start.4) | copy-done | bytes 49176
  5.9 0.0 copy-start.5
  5.9 0.8 %copy-done.5 = bf16[64,384]{1,0:T(8,128)(2,1)S(1)} copy-done((bf16[64,384]{1,0:T(8,128)(2,1)S(1)}, bf16[64,384]{1,0:T(8,128)(2,1)}, u32[]{:S(2)}) %copy-start.5) | copy-done | bytes 49176
  6.7 0.0 copy-start.6
  6.7 0.8 %copy-done.6 = bf16[64,384]{1,0:T(8,128)(2,1)S(1)} copy-done((bf16[64,384]{1,0:T(8,128)(2,1)S(1)}, bf16[64,384]{1,0:T(8,128)(2,1)}, u32[]{:S(2)}) %copy-start.6) | copy-done | bytes 49176
  7.5 0.0 copy-start.7
  7.5 0.7 %copy-done.7 = s32[32,32]{1,0:T(8,128)S(1)} copy-done((s32[32,32]{1,0:T(8,128)S(1)}, s32[32,32]{1,0:T(8,128)}, u32[]{:S(2)}) %copy-start.7) | copy-done | bytes 4120
  8.2 51.2 %shard_map.95 = (bf16[64,384]{1,0:T(8,128)(2,1)S(1)}, bf16[256,384]{1,0:T(8,128)(2,1)S(1)}) custom-call(bf16[64,384]{1,0:T(8,128)(2,1)S(1)} %copy-done.4, bf16[64,384]{1,0:T(8,128)(2,1)S(1)} %copy-done.5, bf16[64,384]{1,0:T(8,128)(2,1)S(1)} %copy-done.6, bf16[256,384]{1,0:T(8,128)(2,1)S(1)} %copy-done.1, bf16[256,384]{1,0:T(8,128)(2,1)S(1)} %copy-done.2, ...), custom_call_target="tpu_custom_call" | custom-call | tf_op jit(solution)/shard_map/pallas_call | solution.py:278
  59.4 0.6 %copy.12 = bf16[64,384]{1,0:T(8,128)(2,1)} copy(bf16[64,384]{1,0:T(8,128)(2,1)S(1)} %get-tuple-element.4) | data formatting | bytes 98304
  60.0 0.7 %copy.13 = bf16[256,384]{1,0:T(8,128)(2,1)} copy(bf16[256,384]{1,0:T(8,128)(2,1)S(1)} %get-tuple-element.5) | data formatting | bytes 393216
Async XLA Ops:
  0.6 1.7 %copy-start = (bf16[384,3072]{1,0:T(8,128)(2,1)S(1)}, bf16[384,3072]{1,0:T(8,128)(2,1)}, u32[]{:S(2)}) copy-start(bf16[384,3072]{1,0:T(8,128)(2,1)} %w.1) | copy-start | bytes 7077892
  2.3 0.9 %copy-start.1 = (bf16[256,384]{1,0:T(8,128)(2,1)S(1)}, bf16[256,384]{1,0:T(8,128)(2,1)}, u32[]{:S(2)}) copy-start(bf16[256,384]{1,0:T(8,128)(2,1)} %tq.1) | copy-start | bytes 589828
  3.2 0.9 %copy-start.2 = (bf16[256,384]{1,0:T(8,128)(2,1)S(1)}, bf16[256,384]{1,0:T(8,128)(2,1)}, u32[]{:S(2)}) copy-start(bf16[256,384]{1,0:T(8,128)(2,1)} %tk.1) | copy-start | bytes 589828
  4.2 0.9 %copy-start.3 = (bf16[256,384]{1,0:T(8,128)(2,1)S(1)}, bf16[256,384]{1,0:T(8,128)(2,1)}, u32[]{:S(2)}) copy-start(bf16[256,384]{1,0:T(8,128)(2,1)} %tv.1) | copy-start | bytes 589828
  5.1 0.8 %copy-start.4 = (bf16[64,384]{1,0:T(8,128)(2,1)S(1)}, bf16[64,384]{1,0:T(8,128)(2,1)}, u32[]{:S(2)}) copy-start(bf16[64,384]{1,0:T(8,128)(2,1)} %vq.1) | copy-start | bytes 147460
  5.9 0.8 %copy-start.5 = (bf16[64,384]{1,0:T(8,128)(2,1)S(1)}, bf16[64,384]{1,0:T(8,128)(2,1)}, u32[]{:S(2)}) copy-start(bf16[64,384]{1,0:T(8,128)(2,1)} %vk.1) | copy-start | bytes 147460
  6.7 0.8 %copy-start.6 = (bf16[64,384]{1,0:T(8,128)(2,1)S(1)}, bf16[64,384]{1,0:T(8,128)(2,1)}, u32[]{:S(2)}) copy-start(bf16[64,384]{1,0:T(8,128)(2,1)} %vv.1) | copy-start | bytes 147460
  7.5 0.7 %copy-start.7 = (s32[32,32]{1,0:T(8,128)S(1)}, s32[32,32]{1,0:T(8,128)}, u32[]{:S(2)}) copy-start(s32[32,32]{1,0:T(8,128)} %mask.1) | copy-start | bytes 12292

commit v2 on v1

v2 whole, which is shorter than its diff:
```python
import functools
import math

import jax
import jax.numpy as jnp
from jax import lax
from jax.experimental import pallas as pl
from jax.experimental.pallas import tpu as pltpu
from jax.sharding import PartitionSpec as P

HEAD_DIM = 128
ROWS = 64
HEADS = 3
NZ, NX, NY = 8, 4, 8
FEATURES = HEADS * HEAD_DIM
TXT_ROWS = 16
TXT_KEYS = 64
TEXT = 64
GROUP = {0: 0, 1: 80, 3: 144, 2: 208}
QUERIES = 272
USED = (272, 272, 208, 208, 80)
STEP_KEYS = 256
NEG = -1e30
SCALE = math.log2(math.e) / math.sqrt(HEAD_DIM)
MESH = pl.DeviceIdType.MESH
BF16, F32 = jnp.bfloat16, jnp.float32


def body(vq, vk, vv, tq, tk, tv, mask, w, out, tout,
         q, kv, tkv, bias, acc, top, osend, orecv, tsend, trecv, attn, wbuf, ysend, yrecv, yterm,
         load_sem, w_sem, q_send, q_recv, z_send, z_recv, s_send, s_recv,
         o_send, o_recv, x_send, x_recv, y_send, y_recv, t_send, t_recv, up_sem, down_sem):
    ctx, y = lax.axis_index("ctx"), lax.axis_index("head")
    core, x, z = ctx % 2, (ctx // 2) % NX, ctx // (2 * NX)
    row_id = 2 * z + core

    def device(zz, xx, cc, yy):
        return ((zz * NX + xx) * 2 + cc, yy)

    def text_device(k):
        other = (row_id + k) % (2 * NZ)
        return device(other // 2, x, other % 2, y)

    up = device((z + 1) % NZ, x, core, y)
    down = device((z + NZ - 1) % NZ, x, core, y)
    sibling = device(z, x, 1 - core, y)

    def x_device(k):
        return device(z, (x + k) % NX, core, y)

    def y_device(k):
        return (ctx, (y + k) % NY)

    def signal(sem, to):
        pl.semaphore_signal(sem, inc=1, device_id=to, device_id_type=MESH)

    barrier = pltpu.get_barrier_semaphore()
    peers = [up, down, sibling] + [x_device(k) for k in range(1, NX)]
    peers += [y_device(1), y_device(NY - 1)]
    for peer in peers:
        signal(barrier, peer)

    loads = []

    def load(src, dst):
        copy = pltpu.make_async_copy(src, dst, load_sem.at[len(loads)])
        copy.start()
        loads.append(copy)

    for h in range(HEADS):
        for part, ref in enumerate((vk, vv)):
            load(ref.at[:, pl.ds(h * HEAD_DIM, HEAD_DIM)], kv.at[h, 0, core, part])
    load(vq, q.at[pl.ds(GROUP[0], ROWS)])
    load(tq.at[pl.ds(row_id * TXT_ROWS, TXT_ROWS)], q.at[pl.ds(TEXT, TXT_ROWS)])
    load(tk.at[pl.ds(x * TXT_KEYS, TXT_KEYS)], tkv.at[0, pl.ds(0, TXT_KEYS)])
    load(tv.at[pl.ds(x * TXT_KEYS, TXT_KEYS)], tkv.at[1, pl.ds(0, TXT_KEYS)])

    sent = []

    def remote(src, dst, send, recv, to):
        return pltpu.make_async_remote_copy(
            src_ref=src, dst_ref=dst, send_sem=send, recv_sem=recv,
            device_id=to, device_id_type=MESH)

    def start(copy):
        copy.start()
        sent.append(copy)

    def z_copy(h, part, direction, d):
        here = d - 1 if direction == 0 else (NZ - d + 1) % NZ
        there = d if direction == 0 else NZ - d
        src = kv.at[h, here, core, part]
        if d == 1:
            src = (vk, vv)[part].at[:, pl.ds(h * HEAD_DIM, HEAD_DIM)]
        sems = (h, part, direction, d - 1)
        return remote(src, kv.at[h, there, core, part], z_send.at[sems], z_recv.at[sems],
                      up if direction == 0 else down)

    def s_copy(h, slot, cc):
        ref = kv.at[h, slot, cc]
        return remote(ref, ref, s_send.at[h, slot], s_recv.at[h, slot], sibling)

    def s_own(h, part, cc):
        index = 0 if part == 0 else NZ
        return remote((vk, vv)[part].at[:, pl.ds(h * HEAD_DIM, HEAD_DIM)], kv.at[h, 0, cc, part],
                      s_send.at[h, index], s_recv.at[h, index], sibling)

    def q_copy(k):
        return remote(vq, q.at[pl.ds(GROUP[NX - k], ROWS)], q_send.at[k], q_recv.at[k], x_device(k))

    pl.semaphore_wait(barrier, len(peers))
    for h in range(HEADS):
        for part in range(2):
            for direction in range(2):
                start(z_copy(h, part, direction, 1))
    for k in (2, 1, 3):
        start(q_copy(k))
    for h in range(HEADS):
        for part in range(2):
            start(s_own(h, part, core))
    signal(up_sem.at[0], y_device(1))
    signal(down_sem.at[0], y_device(NY - 1))
    w_loads = []
    for k in range(NY):
        copy = pltpu.make_async_copy(
            w.at[:, pl.ds(((y + k) % NY) * FEATURES, FEATURES)], wbuf.at[k], w_sem.at[k])
        copy.start()
        w_loads.append(copy)

    for s in range(5):
        for half in range(2):
            cols = slice(half * HEAD_DIM, (half + 1) * HEAD_DIM)
            if half == 1 and s == 4:
                continue
            if half == 1 and s == 0:
                lane = lax.broadcasted_iota(jnp.int32, (QUERIES, HEAD_DIM), 1)
                bias[0, :, cols] = jnp.where(lane < TXT_KEYS, 0.0, NEG).astype(F32)
                continue
            tile_z = (z + NZ - s) % NZ if half == 0 else (z + s) % NZ
            for k in range(NX):
                if GROUP[k] >= USED[s]:
                    continue
                reach = mask[z * NX + (x + k) % NX, tile_z * NX + x].astype(F32)
                bias[s, GROUP[k]:GROUP[k] + ROWS, cols] = jnp.full(
                    (ROWS, HEAD_DIM), (1.0 - reach) * NEG, F32)
            bias[s, TEXT:TEXT + TXT_ROWS, cols] = jnp.zeros((TXT_ROWS, HEAD_DIM), F32)
    for part in range(2):
        tkv[part, TXT_KEYS:] = jnp.zeros((HEAD_DIM - TXT_KEYS, FEATURES), BF16)

    ones = jnp.ones((STEP_KEYS, HEAD_DIM), BF16)

    def absorb(h, s):
        cols = slice(h * HEAD_DIM, (h + 1) * HEAD_DIM)
        slots = {0: (0,), 4: (4,)}.get(s, (s, NZ - s))
        used = USED[s]
        keys = [kv[h, slot, cc, 0] for slot in slots for cc in range(2)]
        values = [kv[h, slot, cc, 1] for slot in slots for cc in range(2)]
        if s == 0:
            keys.append(tkv[0, :, cols])
            values.append(tkv[1, :, cols])
        keys, values = jnp.concatenate(keys, 0), jnp.concatenate(values, 0)
        count = keys.shape[0]
        scores = lax.dot_general(q[:used, cols], keys, (((1,), (1,)), ((), ())),
                                 preferred_element_type=F32)
        scores = scores * SCALE + bias[s, :used, :count]
        high = jnp.max(scores, axis=1, keepdims=True)
        if s:
            before = top[h, :used][:, :1]
            high = jnp.maximum(high, before)
        weights = jnp.exp2(scores - high).astype(BF16)
        values = jnp.concatenate([values, ones[:count]], 1)
        summed = jnp.dot(weights, values, preferred_element_type=F32)
        if s:
            summed = summed + acc[h, :used] * jnp.exp2(before - high)
        acc[h, :used] = summed
        top[h, :used] = jnp.broadcast_to(high, (used, HEAD_DIM))

    def forward(h, d):
        if d < 4:
            for part in range(2):
                for direction in range(2):
                    z_copy(h, part, direction, d).wait_recv()
                    if d < 3 or part == direction:
                        start(z_copy(h, part, direction, d + 1))
            for direction in range(2):
                start(s_copy(h, d if direction == 0 else NZ - d, core))
        else:
            for part in range(2):
                z_copy(h, part, part, 4).wait_recv()
            start(s_copy(h, 4, core))

    def from_sibling(h, s):
        if s == 0:
            for part in range(2):
                s_own(h, part, 1 - core).wait_recv()
        else:
            for slot in (s, NZ - s) if s < 4 else (4,):
                s_copy(h, slot, 1 - core).wait_recv()

    def eye(rows):
        return (lax.broadcasted_iota(jnp.int32, (rows, HEAD_DIM), 0)
                == lax.broadcasted_iota(jnp.int32, (rows, HEAD_DIM), 1))

    def finish(h, first, rows):
        block = slice(first, first + rows)
        total = acc[h, block, HEAD_DIM:]
        return acc[h, block, :HEAD_DIM] / total, top[h, block] + jnp.log2(total)

    def to_rows(level):
        row = jnp.sum(jnp.where(eye(level.shape[0]), level, 0.0), axis=0, keepdims=True)
        first = row.astype(BF16).astype(F32)
        second = (row - first).astype(BF16).astype(F32)
        index = lax.broadcasted_iota(jnp.int32, (16, HEAD_DIM), 0)
        rest = jnp.where(index == 1, second, jnp.where(index == 2, row - first - second, 0.0))
        return jnp.where(index == 0, first, rest).astype(BF16)

    def to_column(rows, count):
        row = rows[0:1] + rows[1:2] + rows[2:3]
        return jnp.sum(jnp.where(eye(count), jnp.broadcast_to(row, (count, HEAD_DIM)), 0.0),
                       axis=1, keepdims=True)

    def o_copy(h, k):
        return remote(osend.at[h, k], orecv.at[h, k], o_send.at[h, k], o_recv.at[h, k], x_device(k))

    def give(h, k):
        block, level = finish(h, GROUP[k], ROWS)
        osend[h, k, :ROWS] = block.astype(BF16)
        osend[h, k, ROWS:] = to_rows(level)
        start(o_copy(h, k))

    def merge(parts, levels):
        high = functools.reduce(jnp.maximum, levels)
        shares = [jnp.exp2(level - high) for level in levels]
        total = functools.reduce(jnp.add, shares)
        return functools.reduce(
            jnp.add, [part * (share / total) for part, share in zip(parts, shares)]).astype(BF16)

    for copy in loads:
        copy.wait()
    for k in (1, 3, 2):
        q_copy(k).wait_recv()
    for h in range(HEADS):
        forward(h, 1)
        from_sibling(h, 0)
        absorb(h, 0)
    for step in range(1, 3):
        pl.semaphore_wait(up_sem.at[step - 1], 1)
        pl.semaphore_wait(down_sem.at[step - 1], 1)
        signal(up_sem.at[step], y_device(1))
        signal(down_sem.at[step], y_device(NY - 1))
    for h in range(HEADS):
        forward(h, 2)
        from_sibling(h, 1)
        absorb(h, 1)
        give(h, 2)
    for h in range(HEADS):
        forward(h, 3)
        from_sibling(h, 2)
        absorb(h, 2)
    for h in range(HEADS):
        from_sibling(h, 3)
        absorb(h, 3)
        give(h, 1)
        give(h, 3)
    for h in range(HEADS):
        forward(h, 4)
    pl.semaphore_wait(up_sem.at[2], 1)
    pl.semaphore_wait(down_sem.at[2], 1)
    for copy in w_loads:
        copy.wait()

    for h in range(HEADS):
        from_sibling(h, 4)
        absorb(h, 4)
        part, level = finish(h, TEXT, TXT_ROWS)
        tsend[h, :TXT_ROWS] = part.astype(BF16)
        tsend[h, TXT_ROWS:] = to_rows(level)

    def x_copy(k):
        return remote(tsend, trecv.at[k], x_send.at[k], x_recv.at[k], x_device(k))

    for k in (2, 1, 3):
        start(x_copy(k))

    for h in range(HEADS):
        part, level = finish(h, GROUP[0], ROWS)
        parts, levels = [part], [level[:, :1]]
        for k in (2, 1, 3):
            o_copy(h, k).wait_recv()
            parts.append(orecv[h, k, :ROWS].astype(F32))
            levels.append(to_column(orecv[h, k, ROWS:].astype(F32), ROWS))
        attn[:, h * HEAD_DIM:(h + 1) * HEAD_DIM] = merge(parts, levels)

    def product(k):
        return jnp.dot(attn[...], wbuf[k], preferred_element_type=F32)

    def y_copy(k):
        to = {3: 1, 5: NY - 1}.get(k, k)
        return remote(ysend.at[k], yrecv.at[k], y_send.at[k], y_recv.at[k], y_device(to))

    for k in (3, 5, 4):
        ysend[k] = product(k).astype(BF16)
        start(y_copy(k))
    for k in (1, 7):
        ysend[k] = product(k).astype(BF16)
    for k, relay in ((2, 3), (6, 5)):
        yterm[...] = product(k)
        y_copy(relay).wait_recv()
        yterm[...] += yrecv[relay].astype(F32)
        ysend[k] = yterm[...].astype(BF16)
        start(y_copy(k))
    for k in (1, 7):
        start(y_copy(k))
    total = product(0)

    mine = pl.ds(pl.multiple_of(row_id * TXT_ROWS, TXT_ROWS), TXT_ROWS)
    for k in (1, 2, 3):
        x_copy(k).wait_recv()
    trecv[0] = tsend[...]
    for h in range(HEADS):
        parts = [trecv[k, h, :TXT_ROWS].astype(F32) for k in range(NX)]
        levels = [to_column(trecv[k, h, TXT_ROWS:].astype(F32), TXT_ROWS) for k in range(NX)]
        tout[mine, h * HEAD_DIM:(h + 1) * HEAD_DIM] = merge(parts, levels)
    for k in range(1, 2 * NZ):
        start(remote(tout.at[mine], tout.at[mine], t_send.at[k], t_recv.at[k], text_device(k)))

    for k in (4, 1, 7, 2, 6):
        y_copy(k).wait_recv()
        total = total + yrecv[k].astype(F32)
    out[...] = total.astype(BF16)

    for k in range(1, 2 * NZ):
        other = (row_id + 2 * NZ - k) % (2 * NZ)
        ref = tout.at[pl.ds(pl.multiple_of(other * TXT_ROWS, TXT_ROWS), TXT_ROWS)]
        remote(ref, ref, t_send.at[k], t_recv.at[k], text_device(k)).wait_recv()
    for copy in sent:
        copy.wait_send()


def local(video_q, video_k, video_v, text_q, text_k, text_v, tile_mask, out_weight):
    hbm = pl.BlockSpec(memory_space=pltpu.HBM)
    vmem = pl.BlockSpec(memory_space=pltpu.VMEM)
    dma = pltpu.SemaphoreType.DMA
    regular = pltpu.SemaphoreType.REGULAR
    return pl.pallas_call(
        body,
        out_shape=(
            jax.ShapeDtypeStruct((ROWS, FEATURES), BF16),
            jax.ShapeDtypeStruct((2 * NZ * TXT_ROWS, FEATURES), BF16),
        ),
        in_specs=[hbm] * 6 + [pl.BlockSpec(memory_space=pltpu.SMEM), hbm],
        out_specs=(vmem, vmem),
        scratch_shapes=[
            pltpu.VMEM((QUERIES, FEATURES), BF16),
            pltpu.VMEM((HEADS, NZ, 2, 2, ROWS, HEAD_DIM), BF16),
            pltpu.VMEM((2, HEAD_DIM, FEATURES), BF16),
            pltpu.VMEM((5, QUERIES, STEP_KEYS), F32),
            pltpu.VMEM((HEADS, QUERIES, 2 * HEAD_DIM), F32),
            pltpu.VMEM((HEADS, QUERIES, HEAD_DIM), F32),
            pltpu.VMEM((HEADS, NX, ROWS + 16, HEAD_DIM), BF16),
            pltpu.VMEM((HEADS, NX, ROWS + 16, HEAD_DIM), BF16),
            pltpu.VMEM((HEADS, TXT_ROWS + 16, HEAD_DIM), BF16),
            pltpu.VMEM((NX, HEADS, TXT_ROWS + 16, HEAD_DIM), BF16),
            pltpu.VMEM((ROWS, FEATURES), BF16),
            pltpu.VMEM((NY, FEATURES, FEATURES), BF16),
            pltpu.VMEM((NY, ROWS, FEATURES), BF16),
            pltpu.VMEM((NY, ROWS, FEATURES), BF16),
            pltpu.VMEM((ROWS, FEATURES), F32),
            dma((10,)),
            dma((NY,)),
            dma((NX,)), dma((NX,)),
            dma((HEADS, 2, 2, 4)), dma((HEADS, 2, 2, 4)),
            dma((HEADS, NZ + 1)), dma((HEADS, NZ + 1)),
            dma((HEADS, NX)), dma((HEADS, NX)),
            dma((NX,)), dma((NX,)),
            dma((NY,)), dma((NY,)),
            dma((2 * NZ,)), dma((2 * NZ,)),
            regular((3,)), regular((3,)),
        ],
        compiler_params=pltpu.CompilerParams(
            collective_id=0, has_side_effects=True, vmem_limit_bytes=60 * 2**20),
    )(video_q, video_k, video_v, text_q, text_k, text_v, tile_mask, out_weight)


def solution(mesh):
    placed = (
        P("ctx", "head"),
        P("ctx", "head"),
        P("ctx", "head"),
        P(None, "head"),
        P(None, "head"),
        P(None, "head"),
        P(),
        P("head", None),
    )
    return jax.shard_map(
        local,
        mesh=mesh,
        in_specs=placed,
        out_specs=(P("ctx", "head"), P(None, "head")),
        check_vma=False,
    )
```

time: 61.1 us -> 51 us (0.83)
  local copies, waits for them, and re-layouts: 8.85 us -> 3.05 us
  Pallas kernels: 51.2 us -> 46.5 us
    unnamed x18 -> x2, local copies, waits for them, and re-layouts: 8.85 us -> 3.05 us
    pallas_call x1, Pallas kernels: 51.2 us -> 46.5 us  [local(): pl.pallas_call(body, out_shape=(jax.ShapeDtypeStruct((ROWS, FEATURES), BF...]
where the time goes in v2:
time: 51 us; the launch traced here: 50.2 us
  Pallas kernels  46.5 us (91%)
  local copies, waits for them, and re-layouts  3.05 us (6%)
  between operations  0.64 us (1%)
    pallas_call x1, Pallas kernels, local(): pl.pallas_call(body, out_shape=(jax.ShapeDtypeStruct((ROWS, FEATURES), BF...  46.5 us
    unnamed x2, local copies, waits for them, and re-layouts  3.05 us

profile of v2, /device:TPU:1, one launch (start us, length us, event | category | flops | bytes accessed | tf_op | source)
XLA Modules:
  0.0 50.2 jit_solution(11324766603721358471)
XLA Ops:
  0.6 46.5 %shard_map.95 = (bf16[64,384]{1,0:T(8,128)(2,1)}, bf16[256,384]{1,0:T(8,128)(2,1)}) custom-call(bf16[64,384]{1,0:T(8,128)(2,1)} %vq.1, bf16[64,384]{1,0:T(8,128)(2,1)} %vk.1, bf16[64,384]{1,0:T(8,128)(2,1)} %vv.1, bf16[256,384]{1,0:T(8,128)(2,1)} %tq.1, bf16[256,384]{1,0:T(8,128)(2,1)} %tk.1, bf16[256,384]{1,0:T(8,128)(2,1)} %tv.1, s32[32,32]{1,0:T(8,128)} %mask.1, ...), custom_call_target="tpu_custom_call" | custom-call | tf_op jit(solution)/shard_map/pallas_call | solution.py:345
  47.1 1.4 %copy.12 = bf16[64,384]{1,0:T(8,128)(2,1)} copy(bf16[64,384]{1,0:T(8,128)(2,1)} %get-tuple-element.4) | data formatting | bytes 98304
  48.5 1.6 %copy.13 = bf16[256,384]{1,0:T(8,128)(2,1)} copy(bf16[256,384]{1,0:T(8,128)(2,1)} %get-tuple-element.5) | data formatting | bytes 393216

commit v3 on v2

v3 whole, which is shorter than its diff:
```python
import functools
import math

import jax
import jax.numpy as jnp
from jax import lax
from jax.experimental import pallas as pl
from jax.experimental.pallas import tpu as pltpu
from jax.sharding import PartitionSpec as P

HEAD_DIM = 128
ROWS = 64
HEADS = 3
NZ, NX, NY = 8, 4, 8
FEATURES = HEADS * HEAD_DIM
TXT_ROWS = 16
TXT_KEYS = 64
TEXT = 64
GROUP = {0: 0, 1: 80, 3: 144, 2: 208}
QUERIES = 272
USED = (272, 272, 208, 208, 80)
STEP_KEYS = 256
TILES = NZ * NX
PLACE = {3: 0, 5: 1, 1: 2, 2: 3, 4: 4, 6: 5, 7: 6}
NEG = -1e30
SCALE = math.log2(math.e) / math.sqrt(HEAD_DIM)
MESH = pl.DeviceIdType.MESH
BF16, F32 = jnp.bfloat16, jnp.float32


def body(vq, vk, vv, tq, tk, tv, mask, w, out, tout,
         q, kv, tkv, bias, acc, top, osend, orecv, tsend, trecv, attn, wbuf, ysend, yrecv, yterm,
         reach, load_sem, send_sem, z_recv, s_recv, o_recv, once_recv, up_sem, down_sem):
    ctx, y = lax.axis_index("ctx"), lax.axis_index("head")
    core, x, z = ctx % 2, (ctx // 2) % NX, ctx // (2 * NX)
    row_id = 2 * z + core

    def device(zz, xx, cc, yy):
        return ((zz * NX + xx) * 2 + cc, yy)

    def text_device(k):
        other = (row_id + k) % (2 * NZ)
        return device(other // 2, x, other % 2, y)

    up = device((z + 1) % NZ, x, core, y)
    down = device((z + NZ - 1) % NZ, x, core, y)
    sibling = device(z, x, 1 - core, y)

    def x_device(k):
        return device(z, (x + k) % NX, core, y)

    def y_device(k):
        return (ctx, (y + k) % NY)

    def signal(sem, to):
        pl.semaphore_signal(sem, inc=1, device_id=to, device_id_type=MESH)

    barrier = pltpu.get_barrier_semaphore()
    peers = [up, down, sibling] + [x_device(k) for k in range(1, NX)]
    peers += [y_device(1), y_device(NY - 1)]
    for peer in peers:
        signal(barrier, peer)

    def load(src, dst, sem):
        pltpu.make_async_copy(src, dst, load_sem.at[sem]).start()

    def take(ref, sem):
        pltpu.make_async_copy(ref, ref, sem).wait()

    def remote(src, dst, send, recv, to):
        return pltpu.make_async_remote_copy(
            src_ref=src, dst_ref=dst, send_sem=send, recv_sem=recv,
            device_id=to, device_id_type=MESH)

    def slot(direction, d):
        return {0: 0, 4: 1}.get(d, 2 * d + direction)

    def z_copy(h, part, direction, d):
        src = kv.at[h, slot(direction, d - 1), core]
        dst = kv.at[h, slot(direction, d), core]
        if part is not None:
            src, dst = src.at[part], dst.at[part]
        if d == 1:
            src = (vk, vv)[part].at[:, pl.ds(h * HEAD_DIM, HEAD_DIM)]
        return remote(src, dst, send_sem.at[0], z_recv.at[h, direction, d - 1],
                      up if direction == 0 else down)

    def s_copy(h, place, step):
        ref = kv.at[h, place, core]
        return remote(ref, ref, send_sem.at[1], s_recv.at[h, step], sibling)

    def s_own(h, part):
        return remote((vk, vv)[part].at[:, pl.ds(h * HEAD_DIM, HEAD_DIM)], kv.at[h, 0, core, part],
                      send_sem.at[1], s_recv.at[h, 0], sibling)

    def q_copy(k):
        return remote(vq, q.at[pl.ds(GROUP[NX - k], ROWS)], send_sem.at[2], once_recv.at[0],
                      x_device(k))

    pl.semaphore_wait(barrier, len(peers))
    for h in range(HEADS):
        for direction in range(2):
            z_copy(h, 0, direction, 1).start()
            z_copy(h, 1, direction, 1).start()
    for k in (2, 1, 3):
        q_copy(k).start()
    for h in range(HEADS):
        for part in range(2):
            s_own(h, part).start()
    load(mask, reach, 0)
    for h in range(HEADS):
        for part, ref in enumerate((vk, vv)):
            load(ref.at[:, pl.ds(h * HEAD_DIM, HEAD_DIM)], kv.at[h, 0, core, part], 1)
    load(vq, q.at[pl.ds(GROUP[0], ROWS)], 2)
    load(tq.at[pl.ds(row_id * TXT_ROWS, TXT_ROWS)], q.at[pl.ds(TEXT, TXT_ROWS)], 3)
    for part, ref in enumerate((tk, tv)):
        load(ref.at[pl.ds(x * TXT_KEYS, TXT_KEYS)], tkv.at[part, pl.ds(0, TXT_KEYS)], 4)
    signal(up_sem.at[0], y_device(1))
    signal(down_sem.at[0], y_device(NY - 1))
    for k in range(NY):
        load(w.at[:, pl.ds(((y + k) % NY) * FEATURES, FEATURES)], wbuf.at[k], 5)
    take(reach, load_sem.at[0])

    for s in range(5):
        for half in range(2):
            cols = slice(half * HEAD_DIM, (half + 1) * HEAD_DIM)
            if half == 1 and s == 4:
                continue
            if half == 1 and s == 0:
                lane = lax.broadcasted_iota(jnp.int32, (QUERIES, HEAD_DIM), 1)
                bias[0, :, cols] = jnp.where(lane < TXT_KEYS, 0.0, NEG).astype(F32)
                continue
            tile_z = (z + NZ - s) % NZ if half == 0 else (z + s) % NZ
            for k in range(NX):
                if GROUP[k] >= USED[s]:
                    continue
                allowed = reach[z * NX + (x + k) % NX, tile_z * NX + x].astype(F32)
                bias[s, GROUP[k]:GROUP[k] + ROWS, cols] = jnp.full(
                    (ROWS, HEAD_DIM), (1.0 - allowed) * NEG, F32)
            bias[s, TEXT:TEXT + TXT_ROWS, cols] = jnp.zeros((TXT_ROWS, HEAD_DIM), F32)
    for part in range(2):
        tkv[part, TXT_KEYS:] = jnp.zeros((HEAD_DIM - TXT_KEYS, FEATURES), BF16)

    ones = jnp.ones((STEP_KEYS, HEAD_DIM), BF16)

    def absorb(h, s):
        cols = slice(h * HEAD_DIM, (h + 1) * HEAD_DIM)
        slots = {0: (0,), 4: (1,)}.get(s, (2 * s, 2 * s + 1))
        used = USED[s]
        keys = [kv[h, slot, cc, 0] for slot in slots for cc in range(2)]
        values = [kv[h, slot, cc, 1] for slot in slots for cc in range(2)]
        if s == 0:
            keys.append(tkv[0, :, cols])
            values.append(tkv[1, :, cols])
        keys, values = jnp.concatenate(keys, 0), jnp.concatenate(values, 0)
        count = keys.shape[0]
        scores = lax.dot_general(q[:used, cols], keys, (((1,), (1,)), ((), ())),
                                 preferred_element_type=F32)
        scores = scores * SCALE + bias[s, :used, :count]
        high = jnp.max(scores, axis=1, keepdims=True)
        if s:
            before = top[h, :used][:, :1]
            high = jnp.maximum(high, before)
        weights = jnp.exp2(scores - high).astype(BF16)
        values = jnp.concatenate([values, ones[:count]], 1)
        summed = jnp.dot(weights, values, preferred_element_type=F32)
        if s:
            summed = summed + acc[h, :used] * jnp.exp2(before - high)
        acc[h, :used] = summed
        top[h, :used] = jnp.broadcast_to(high, (used, HEAD_DIM))

    def forward(h, d):
        for direction in range(2):
            if d < 4:
                ref = kv.at[h, slot(direction, d), core]
            else:
                ref = kv.at[h, 1, core, direction]
            take(ref, z_recv.at[h, direction, d - 1])
            if d < 4:
                z_copy(h, direction if d == 3 else None, direction, d + 1).start()
        for place in (slot(0, d), slot(1, d)) if d < 4 else (1,):
            s_copy(h, place, d).start()

    def from_sibling(h, s):
        places = {0: 0, 4: 1}.get(s, pl.ds(2 * s, 2))
        take(kv.at[h, places, 1 - core], s_recv.at[h, s])

    def eye(rows):
        return (lax.broadcasted_iota(jnp.int32, (rows, HEAD_DIM), 0)
                == lax.broadcasted_iota(jnp.int32, (rows, HEAD_DIM), 1))

    def finish(h, first, rows):
        block = slice(first, first + rows)
        total = acc[h, block, HEAD_DIM:]
        return acc[h, block, :HEAD_DIM] / total, top[h, block] + jnp.log2(total)

    def to_rows(level):
        row = jnp.sum(jnp.where(eye(level.shape[0]), level, 0.0), axis=0, keepdims=True)
        first = row.astype(BF16).astype(F32)
        second = (row - first).astype(BF16).astype(F32)
        index = lax.broadcasted_iota(jnp.int32, (16, HEAD_DIM), 0)
        rest = jnp.where(index == 1, second, jnp.where(index == 2, row - first - second, 0.0))
        return jnp.where(index == 0, first, rest).astype(BF16)

    def to_column(rows, count):
        row = rows[0:1] + rows[1:2] + rows[2:3]
        return jnp.sum(jnp.where(eye(count), jnp.broadcast_to(row, (count, HEAD_DIM)), 0.0),
                       axis=1, keepdims=True)

    def o_copy(h, k):
        return remote(osend.at[h, k - 1], orecv.at[h, k - 1], send_sem.at[3], o_recv.at[h, k - 1],
                      x_device(k))

    def give(h, k):
        block, level = finish(h, GROUP[k], ROWS)
        osend[h, k - 1, :ROWS] = block.astype(BF16)
        osend[h, k - 1, ROWS:] = to_rows(level)
        o_copy(h, k).start()

    def merge(parts, levels):
        high = functools.reduce(jnp.maximum, levels)
        shares = [jnp.exp2(level - high) for level in levels]
        total = functools.reduce(jnp.add, shares)
        return functools.reduce(
            jnp.add, [part * (share / total) for part, share in zip(parts, shares)]).astype(BF16)

    take(kv.at[:, 0, core], load_sem.at[1])
    take(q.at[pl.ds(GROUP[0], ROWS)], load_sem.at[2])
    take(q.at[pl.ds(TEXT, TXT_ROWS)], load_sem.at[3])
    take(tkv.at[:, pl.ds(0, TXT_KEYS)], load_sem.at[4])
    take(q.at[pl.ds(GROUP[1], 3 * ROWS)], once_recv.at[0])
    for h in range(HEADS):
        forward(h, 1)
        from_sibling(h, 0)
        absorb(h, 0)
    for step in range(1, 3):
        pl.semaphore_wait(up_sem.at[step - 1], 1)
        pl.semaphore_wait(down_sem.at[step - 1], 1)
        signal(up_sem.at[step], y_device(1))
        signal(down_sem.at[step], y_device(NY - 1))
    for h in range(HEADS):
        forward(h, 2)
        from_sibling(h, 1)
        absorb(h, 1)
        give(h, 2)
    for h in range(HEADS):
        forward(h, 3)
        from_sibling(h, 2)
        absorb(h, 2)
    for h in range(HEADS):
        from_sibling(h, 3)
        absorb(h, 3)
        give(h, 1)
        give(h, 3)
    for h in range(HEADS):
        forward(h, 4)
    pl.semaphore_wait(up_sem.at[2], 1)
    pl.semaphore_wait(down_sem.at[2], 1)
    take(wbuf, load_sem.at[5])

    for h in range(HEADS):
        from_sibling(h, 4)
    for h in range(HEADS):
        absorb(h, 4)
    for h in range(HEADS):
        for k in range(1, NX):
            o_copy(h, k).wait_recv()

    for h in range(HEADS):
        part, level = finish(h, GROUP[0], ROWS)
        parts, levels = [part], [level[:, :1]]
        for k in range(1, NX):
            parts.append(orecv[h, k - 1, :ROWS].astype(F32))
            levels.append(to_column(orecv[h, k - 1, ROWS:].astype(F32), ROWS))
        attn[:, h * HEAD_DIM:(h + 1) * HEAD_DIM] = merge(parts, levels)

    def product(k):
        return jnp.dot(attn[...], wbuf[k], preferred_element_type=F32)

    def y_copy(k):
        to = {3: 1, 5: NY - 1}.get(k, k)
        return remote(ysend.at[PLACE[k]], yrecv.at[PLACE[k]], send_sem.at[5],
                      once_recv.at[{3: 2, 5: 3}.get(k, 4)], y_device(to))

    for k in (3, 5, 4, 1, 7):
        ysend[PLACE[k]] = product(k).astype(BF16)
        y_copy(k).start()

    def x_copy(k):
        return remote(tsend, trecv.at[k], send_sem.at[4], once_recv.at[1], x_device(k))

    for h in range(HEADS):
        part, level = finish(h, TEXT, TXT_ROWS)
        tsend[h, :TXT_ROWS] = part.astype(BF16)
        tsend[h, TXT_ROWS:] = to_rows(level)
    for k in (2, 1, 3):
        x_copy(k).start()
    for k, relay in ((2, 3), (6, 5)):
        yterm[...] = product(k)
        y_copy(relay).wait_recv()
        yterm[...] += yrecv[PLACE[relay]].astype(F32)
        ysend[PLACE[k]] = yterm[...].astype(BF16)
        y_copy(k).start()
    total = product(0)

    mine = pl.ds(pl.multiple_of(row_id * TXT_ROWS, TXT_ROWS), TXT_ROWS)
    take(trecv.at[pl.ds(1, NX - 1)], once_recv.at[1])
    trecv[0] = tsend[...]
    for h in range(HEADS):
        parts = [trecv[k, h, :TXT_ROWS].astype(F32) for k in range(NX)]
        levels = [to_column(trecv[k, h, TXT_ROWS:].astype(F32), TXT_ROWS) for k in range(NX)]
        tout[mine, h * HEAD_DIM:(h + 1) * HEAD_DIM] = merge(parts, levels)
    for k in range(1, 2 * NZ):
        remote(tout.at[mine], tout.at[mine], send_sem.at[6], once_recv.at[5], text_device(k)).start()

    take(yrecv.at[pl.ds(2, 5)], once_recv.at[4])
    for k in (1, 2, 4, 6, 7):
        total = total + yrecv[PLACE[k]].astype(F32)
    out[...] = total.astype(BF16)

    rest = tout.at[pl.ds(0, (2 * NZ - 1) * TXT_ROWS)]
    take(rest, once_recv.at[5])
    for index, ref in enumerate((kv.at[:, pl.ds(0, 7), 0], kv.at[:, :, 0],
                                 q.at[pl.ds(GROUP[1], 3 * ROWS)], osend,
                                 trecv.at[pl.ds(1, NX - 1)], ysend, rest)):
        take(ref, send_sem.at[index])


def local(video_q, video_k, video_v, text_q, text_k, text_v, tile_mask, out_weight):
    hbm = pl.BlockSpec(memory_space=pltpu.HBM)
    vmem = pl.BlockSpec(memory_space=pltpu.VMEM)
    dma = pltpu.SemaphoreType.DMA
    in_hbm = functools.partial(pltpu.with_memory_space_constraint, memory_space=pltpu.HBM)
    regular = pltpu.SemaphoreType.REGULAR
    return pl.pallas_call(
        body,
        out_shape=(
            jax.ShapeDtypeStruct((ROWS, FEATURES), BF16),
            jax.ShapeDtypeStruct((2 * NZ * TXT_ROWS, FEATURES), BF16),
        ),
        in_specs=[hbm] * 6 + [hbm, hbm],
        out_specs=(vmem, vmem),
        scratch_shapes=[
            pltpu.VMEM((QUERIES, FEATURES), BF16),
            pltpu.VMEM((HEADS, NZ, 2, 2, ROWS, HEAD_DIM), BF16),
            pltpu.VMEM((2, HEAD_DIM, FEATURES), BF16),
            pltpu.VMEM((5, QUERIES, STEP_KEYS), F32),
            pltpu.VMEM((HEADS, QUERIES, 2 * HEAD_DIM), F32),
            pltpu.VMEM((HEADS, QUERIES, HEAD_DIM), F32),
            pltpu.VMEM((HEADS, NX - 1, ROWS + 16, HEAD_DIM), BF16),
            pltpu.VMEM((HEADS, NX - 1, ROWS + 16, HEAD_DIM), BF16),
            pltpu.VMEM((HEADS, TXT_ROWS + 16, HEAD_DIM), BF16),
            pltpu.VMEM((NX, HEADS, TXT_ROWS + 16, HEAD_DIM), BF16),
            pltpu.VMEM((ROWS, FEATURES), BF16),
            pltpu.VMEM((NY, FEATURES, FEATURES), BF16),
            pltpu.VMEM((NY - 1, ROWS, FEATURES), BF16),
            pltpu.VMEM((NY - 1, ROWS, FEATURES), BF16),
            pltpu.VMEM((ROWS, FEATURES), F32),
            pltpu.SMEM((TILES, TILES), jnp.int32),
            dma((6,)),
            dma((7,)),
            dma((HEADS, 2, 4)),
            dma((HEADS, 5)),
            dma((HEADS, NX - 1)),
            dma((6,)),
            regular((3,)), regular((3,)),
        ],
        compiler_params=pltpu.CompilerParams(
            collective_id=0, has_side_effects=True, vmem_limit_bytes=40 * 2**20),
    )(*map(in_hbm, (video_q, video_k, video_v, text_q, text_k, text_v, tile_mask, out_weight)))


def solution(mesh):
    placed = (
        P("ctx", "head"),
        P("ctx", "head"),
        P("ctx", "head"),
        P(None, "head"),
        P(None, "head"),
        P(None, "head"),
        P(),
        P("head", None),
    )
    return jax.shard_map(
        local,
        mesh=mesh,
        in_specs=placed,
        out_specs=(P("ctx", "head"), P(None, "head")),
        check_vma=False,
    )
```

time: 51 us -> 45 us (0.88); the launches traced: 50.2 us -> 44.8 us
  Pallas kernels: 46.5 us -> 42.8 us
  local copies, waits for them, and re-layouts: 3.05 us -> 1.3 us
    pallas_call x1, Pallas kernels: 46.5 us -> 42.8 us  [local(): pl.pallas_call(body, out_shape=(jax.ShapeDtypeStruct((ROWS, FEATURES), BF...]
    unnamed x2, local copies, waits for them, and re-layouts: 3.05 us -> 1.3 us
where the time goes in v3:
time: 45 us; the launch traced here: 44.8 us
  Pallas kernels  42.8 us (95%)
  local copies, waits for them, and re-layouts  1.3 us (3%)
  between operations  0.64 us (1%)
    pallas_call x1, Pallas kernels, local(): pl.pallas_call(body, out_shape=(jax.ShapeDtypeStruct((ROWS, FEATURES), BF...  42.8 us
    unnamed x2, local copies, waits for them, and re-layouts  1.3 us

profile of v3, /device:TPU:1, one launch (start us, length us, event | category | flops | bytes accessed | tf_op | source)
XLA Modules:
  0.0 44.8 jit_solution(6070364579831932544)
XLA Ops:
  0.6 42.8 %shard_map.95 = (bf16[64,384]{1,0:T(8,128)(2,1)S(1)}, bf16[256,384]{1,0:T(8,128)(2,1)S(1)}) custom-call(bf16[64,384]{1,0:T(8,128)(2,1)} %vq.1, bf16[64,384]{1,0:T(8,128)(2,1)} %vk.1, bf16[64,384]{1,0:T(8,128)(2,1)} %vv.1, bf16[256,384]{1,0:T(8,128)(2,1)} %tq.1, bf16[256,384]{1,0:T(8,128)(2,1)} %tk.1, bf16[256,384]{1,0:T(8,128)(2,1)} %tv.1, s32[32,32]{1,0:T(8,128)} %mask.1, ...), custom_call_target="tpu_custom_call" | custom-call | tf_op jit(solution)/shard_map/pallas_call | solution.py:335
  43.5 0.6 %copy.12 = bf16[64,384]{1,0:T(8,128)(2,1)} copy(bf16[64,384]{1,0:T(8,128)(2,1)S(1)} %get-tuple-element.4) | data formatting | bytes 98304
  44.1 0.7 %copy.13 = bf16[256,384]{1,0:T(8,128)(2,1)} copy(bf16[256,384]{1,0:T(8,128)(2,1)S(1)} %get-tuple-element.5) | data formatting | bytes 393216

commit v4 on v3

--- a/solution.py
+++ b/solution.py
@@ -217,6 +217,19 @@
         osend[h, k - 1, ROWS:] = to_rows(level)
         o_copy(h, k).start()
 
+    def fold(h):
+        own = slice(GROUP[0], GROUP[0] + ROWS)
+        before = top[h, own][:, :1]
+        parts, levels = [acc[h, own]], [before]
+        for k in range(1, NX):
+            part = orecv[h, k - 1, :ROWS].astype(F32)
+            parts.append(jnp.concatenate([part, jnp.ones((ROWS, HEAD_DIM), F32)], 1))
+            levels.append(to_column(orecv[h, k - 1, ROWS:].astype(F32), ROWS))
+        high = functools.reduce(jnp.maximum, levels)
+        acc[h, own] = functools.reduce(
+            jnp.add, [part * jnp.exp2(level - high) for part, level in zip(parts, levels)])
+        top[h, own] = jnp.broadcast_to(high, (ROWS, HEAD_DIM))
+
     def merge(parts, levels):
         high = functools.reduce(jnp.maximum, levels)
         shares = [jnp.exp2(level - high) for level in levels]
@@ -224,29 +237,33 @@
         return functools.reduce(
             jnp.add, [part * (share / total) for part, share in zip(parts, shares)]).astype(BF16)
 
+    for h in range(HEADS):
+        forward(h, 1)
     take(kv.at[:, 0, core], load_sem.at[1])
     take(q.at[pl.ds(GROUP[0], ROWS)], load_sem.at[2])
     take(q.at[pl.ds(TEXT, TXT_ROWS)], load_sem.at[3])
     take(tkv.at[:, pl.ds(0, TXT_KEYS)], load_sem.at[4])
     take(q.at[pl.ds(GROUP[1], 3 * ROWS)], once_recv.at[0])
     for h in range(HEADS):
-        forward(h, 1)
         from_sibling(h, 0)
         absorb(h, 0)
-    for step in range(1, 3):
-        pl.semaphore_wait(up_sem.at[step - 1], 1)
-        pl.semaphore_wait(down_sem.at[step - 1], 1)
-        signal(up_sem.at[step], y_device(1))
-        signal(down_sem.at[step], y_device(NY - 1))
     for h in range(HEADS):
         forward(h, 2)
         from_sibling(h, 1)
         absorb(h, 1)
         give(h, 2)
+    pl.semaphore_wait(up_sem.at[0], 1)
+    pl.semaphore_wait(down_sem.at[0], 1)
+    signal(up_sem.at[1], y_device(1))
+    signal(down_sem.at[1], y_device(NY - 1))
     for h in range(HEADS):
         forward(h, 3)
         from_sibling(h, 2)
         absorb(h, 2)
+    pl.semaphore_wait(up_sem.at[1], 1)
+    pl.semaphore_wait(down_sem.at[1], 1)
+    signal(up_sem.at[2], y_device(1))
+    signal(down_sem.at[2], y_device(NY - 1))
     for h in range(HEADS):
         from_sibling(h, 3)
         absorb(h, 3)
@@ -259,20 +276,18 @@
     take(wbuf, load_sem.at[5])
 
     for h in range(HEADS):
-        from_sibling(h, 4)
-    for h in range(HEADS):
-        absorb(h, 4)
-    for h in range(HEADS):
         for k in range(1, NX):
             o_copy(h, k).wait_recv()
-
-    for h in range(HEADS):
-        part, level = finish(h, GROUP[0], ROWS)
-        parts, levels = [part], [level[:, :1]]
-        for k in range(1, NX):
-            parts.append(orecv[h, k - 1, :ROWS].astype(F32))
-            levels.append(to_column(orecv[h, k - 1, ROWS:].astype(F32), ROWS))
-        attn[:, h * HEAD_DIM:(h + 1) * HEAD_DIM] = merge(parts, levels)
+    for h in range(HEADS):
+        fold(h)
+    for h in range(HEADS):
+        from_sibling(h, 4)
+    for h in range(HEADS):
+        absorb(h, 4)
+    own = slice(GROUP[0], GROUP[0] + ROWS)
+    for h in range(HEADS):
+        attn[:, h * HEAD_DIM:(h + 1) * HEAD_DIM] = (
+            acc[h, own, :HEAD_DIM] / acc[h, own, HEAD_DIM:]).astype(BF16)
 
     def product(k):
         return jnp.dot(attn[...], wbuf[k], preferred_element_type=F32)

time: 45 us -> 44.6 us (level)
  no operation moved by 1% of the time
where the time goes in v4:
time: 44.6 us; the launch traced here: 44.4 us
  Pallas kernels  42.5 us (95%)
  local copies, waits for them, and re-layouts  1.3 us (3%)
  between operations  0.64 us (1%)
    pallas_call x1, Pallas kernels, local(): pl.pallas_call(body, out_shape=(jax.ShapeDtypeStruct((ROWS, FEATURES), BF...  42.5 us
    unnamed x2, local copies, waits for them, and re-layouts  1.3 us

profile of v4, /device:TPU:1, one launch (start us, length us, event | category | flops | bytes accessed | tf_op | source)
XLA Modules:
  0.0 44.4 jit_solution(7420814686306368460)
XLA Ops:
  0.6 42.5 %shard_map.95 = (bf16[64,384]{1,0:T(8,128)(2,1)S(1)}, bf16[256,384]{1,0:T(8,128)(2,1)S(1)}) custom-call(bf16[64,384]{1,0:T(8,128)(2,1)} %vq.1, bf16[64,384]{1,0:T(8,128)(2,1)} %vk.1, bf16[64,384]{1,0:T(8,128)(2,1)} %vv.1, bf16[256,384]{1,0:T(8,128)(2,1)} %tq.1, bf16[256,384]{1,0:T(8,128)(2,1)} %tk.1, bf16[256,384]{1,0:T(8,128)(2,1)} %tv.1, s32[32,32]{1,0:T(8,128)} %mask.1, ...), custom_call_target="tpu_custom_call" | custom-call | tf_op jit(solution)/shard_map/pallas_call | solution.py:350
  43.1 0.6 %copy.12 = bf16[64,384]{1,0:T(8,128)(2,1)} copy(bf16[64,384]{1,0:T(8,128)(2,1)S(1)} %get-tuple-element.4) | data formatting | bytes 98304
  43.7 0.7 %copy.13 = bf16[256,384]{1,0:T(8,128)(2,1)} copy(bf16[256,384]{1,0:T(8,128)(2,1)S(1)} %get-tuple-element.5) | data formatting | bytes 393216

commit v5 on v4

--- a/solution.py
+++ b/solution.py
@@ -17,11 +17,12 @@
 TXT_KEYS = 64
 TEXT = 64
 GROUP = {0: 0, 1: 80, 3: 144, 2: 208}
-QUERIES = 272
-USED = (272, 272, 208, 208, 80)
+FAR = 272
+QUERIES = 288
+USED = (288, 272, 208, 208, 64)
 STEP_KEYS = 256
 TILES = NZ * NX
-PLACE = {3: 0, 5: 1, 1: 2, 2: 3, 4: 4, 6: 5, 7: 6}
+PLACE = {3: 0, 5: 1, 4: 2, 1: 3, 2: 4, 6: 5, 7: 6}
 NEG = -1e30
 SCALE = math.log2(math.e) / math.sqrt(HEAD_DIM)
 MESH = pl.DeviceIdType.MESH
@@ -29,18 +30,14 @@
 
 
 def body(vq, vk, vv, tq, tk, tv, mask, w, out, tout,
-         q, kv, tkv, bias, acc, top, osend, orecv, tsend, trecv, attn, wbuf, ysend, yrecv, yterm,
-         reach, load_sem, send_sem, z_recv, s_recv, o_recv, once_recv, up_sem, down_sem):
+         q, kv, tkv, bias, acc, top, osend, orecv, tsend, trecv, fsend, frecv, attn, wbuf, ysend, yrecv, yterm,
+         reach, load_sem, send_sem, z_recv, s_recv, o_recv, once_recv, relay_recv, up_sem, down_sem):
     ctx, y = lax.axis_index("ctx"), lax.axis_index("head")
     core, x, z = ctx % 2, (ctx // 2) % NX, ctx // (2 * NX)
     row_id = 2 * z + core
 
     def device(zz, xx, cc, yy):
         return ((zz * NX + xx) * 2 + cc, yy)
-
-    def text_device(k):
-        other = (row_id + k) % (2 * NZ)
-        return device(other // 2, x, other % 2, y)
 
     up = device((z + 1) % NZ, x, core, y)
     down = device((z + NZ - 1) % NZ, x, core, y)
@@ -113,10 +110,14 @@
             load(ref.at[:, pl.ds(h * HEAD_DIM, HEAD_DIM)], kv.at[h, 0, core, part], 1)
     load(vq, q.at[pl.ds(GROUP[0], ROWS)], 2)
     load(tq.at[pl.ds(row_id * TXT_ROWS, TXT_ROWS)], q.at[pl.ds(TEXT, TXT_ROWS)], 3)
+    far_id = (row_id + NZ) % (2 * NZ)
+    load(tq.at[pl.ds(far_id * TXT_ROWS, TXT_ROWS)], q.at[pl.ds(FAR, TXT_ROWS)], 6)
     for part, ref in enumerate((tk, tv)):
         load(ref.at[pl.ds(x * TXT_KEYS, TXT_KEYS)], tkv.at[part, pl.ds(0, TXT_KEYS)], 4)
     signal(up_sem.at[0], y_device(1))
     signal(down_sem.at[0], y_device(NY - 1))
+    signal(up_sem.at[3], up)
+    signal(down_sem.at[3], down)
     for k in range(NY):
         load(w.at[:, pl.ds(((y + k) % NY) * FEATURES, FEATURES)], wbuf.at[k], 5)
     take(reach, load_sem.at[0])
@@ -128,7 +129,8 @@
                 continue
             if half == 1 and s == 0:
                 lane = lax.broadcasted_iota(jnp.int32, (QUERIES, HEAD_DIM), 1)
-                bias[0, :, cols] = jnp.where(lane < TXT_KEYS, 0.0, NEG).astype(F32)
+                row = lax.broadcasted_iota(jnp.int32, (QUERIES, HEAD_DIM), 0)
+                bias[0, :, cols] = jnp.where((lane < TXT_KEYS) & (row < FAR), 0.0, NEG).astype(F32)
                 continue
             tile_z = (z + NZ - s) % NZ if half == 0 else (z + s) % NZ
             for k in range(NX):
@@ -137,10 +139,19 @@
                 allowed = reach[z * NX + (x + k) % NX, tile_z * NX + x].astype(F32)
                 bias[s, GROUP[k]:GROUP[k] + ROWS, cols] = jnp.full(
                     (ROWS, HEAD_DIM), (1.0 - allowed) * NEG, F32)
-            bias[s, TEXT:TEXT + TXT_ROWS, cols] = jnp.zeros((TXT_ROWS, HEAD_DIM), F32)
+            for first in (TEXT, FAR):
+                if first < USED[s]:
+                    bias[s, first:first + TXT_ROWS, cols] = jnp.zeros((TXT_ROWS, HEAD_DIM), F32)
     for part in range(2):
         tkv[part, TXT_KEYS:] = jnp.zeros((HEAD_DIM - TXT_KEYS, FEATURES), BF16)
 
+    def pass_on(sem):
+        pl.semaphore_wait(up_sem.at[sem - 1], 1)
+        pl.semaphore_wait(down_sem.at[sem - 1], 1)
+        signal(up_sem.at[sem], up)
+        signal(down_sem.at[sem], down)
+
+    pass_on(4)
     ones = jnp.ones((STEP_KEYS, HEAD_DIM), BF16)
 
     def absorb(h, s):
@@ -217,18 +228,23 @@
         osend[h, k - 1, ROWS:] = to_rows(level)
         o_copy(h, k).start()
 
-    def fold(h):
-        own = slice(GROUP[0], GROUP[0] + ROWS)
-        before = top[h, own][:, :1]
-        parts, levels = [acc[h, own]], [before]
-        for k in range(1, NX):
-            part = orecv[h, k - 1, :ROWS].astype(F32)
-            parts.append(jnp.concatenate([part, jnp.ones((ROWS, HEAD_DIM), F32)], 1))
-            levels.append(to_column(orecv[h, k - 1, ROWS:].astype(F32), ROWS))
+    def fold(h, first, rows, sources):
+        block = slice(first, first + rows)
+        before = top[h, block][:, :1]
+        parts, levels = [acc[h, block]], [before]
+        for source in sources:
+            part = source[:rows].astype(F32)
+            parts.append(jnp.concatenate([part, jnp.ones((rows, HEAD_DIM), F32)], 1))
+            levels.append(to_column(source[rows:].astype(F32), rows))
         high = functools.reduce(jnp.maximum, levels)
-        acc[h, own] = functools.reduce(
+        acc[h, block] = functools.reduce(
             jnp.add, [part * jnp.exp2(level - high) for part, level in zip(parts, levels)])
-        top[h, own] = jnp.broadcast_to(high, (ROWS, HEAD_DIM))
+        top[h, block] = jnp.broadcast_to(high, (rows, HEAD_DIM))
+
+    def pack_text(h, first, to):
+        part, level = finish(h, first, TXT_ROWS)
+        to[h, :TXT_ROWS] = part.astype(BF16)
+        to[h, TXT_ROWS:] = to_rows(level)
 
     def merge(parts, levels):
         high = functools.reduce(jnp.maximum, levels)
@@ -239,14 +255,21 @@
 
     for h in range(HEADS):
         forward(h, 1)
+    pass_on(5)
     take(kv.at[:, 0, core], load_sem.at[1])
     take(q.at[pl.ds(GROUP[0], ROWS)], load_sem.at[2])
     take(q.at[pl.ds(TEXT, TXT_ROWS)], load_sem.at[3])
+    take(q.at[pl.ds(FAR, TXT_ROWS)], load_sem.at[6])
     take(tkv.at[:, pl.ds(0, TXT_KEYS)], load_sem.at[4])
     take(q.at[pl.ds(GROUP[1], 3 * ROWS)], once_recv.at[0])
     for h in range(HEADS):
         from_sibling(h, 0)
         absorb(h, 0)
+    for h in range(HEADS):
+        pack_text(h, FAR, fsend)
+    pl.semaphore_wait(up_sem.at[5], 1)
+    pl.semaphore_wait(down_sem.at[5], 1)
+    remote(fsend, frecv, send_sem.at[7], once_recv.at[6], device((z + 4) % NZ, x, core, y)).start()
     for h in range(HEADS):
         forward(h, 2)
         from_sibling(h, 1)
@@ -269,6 +292,17 @@
         absorb(h, 3)
         give(h, 1)
         give(h, 3)
+
+    def x_copy(k):
+        return remote(tsend, trecv.at[k], send_sem.at[4], once_recv.at[1], x_device(k))
+
+    take(frecv, once_recv.at[6])
+    for h in range(HEADS):
+        fold(h, TEXT, TXT_ROWS, [frecv.at[h]])
+    for h in range(HEADS):
+        pack_text(h, TEXT, tsend)
+    for k in (2, 1, 3):
+        x_copy(k).start()
     for h in range(HEADS):
         forward(h, 4)
     pl.semaphore_wait(up_sem.at[2], 1)
@@ -279,7 +313,7 @@
         for k in range(1, NX):
             o_copy(h, k).wait_recv()
     for h in range(HEADS):
-        fold(h)
+        fold(h, GROUP[0], ROWS, [orecv.at[h, k - 1] for k in range(1, NX)])
     for h in range(HEADS):
         from_sibling(h, 4)
     for h in range(HEADS):
@@ -292,52 +326,67 @@
     def product(k):
         return jnp.dot(attn[...], wbuf[k], preferred_element_type=F32)
 
-    def y_copy(k):
-        to = {3: 1, 5: NY - 1}.get(k, k)
-        return remote(ysend.at[PLACE[k]], yrecv.at[PLACE[k]], send_sem.at[5],
-                      once_recv.at[{3: 2, 5: 3}.get(k, 4)], y_device(to))
-
-    for k in (3, 5, 4, 1, 7):
+    halves = (slice(0, ROWS // 2), slice(ROWS // 2, ROWS))
+
+    def y_copy(k, half=None, way=0):
+        to = {3: 1, 5: NY - 1, 4: (2, NY - 2)[way]}.get(k, k)
+        src, dst, sem = ysend.at[PLACE[k]], yrecv.at[PLACE[k]], once_recv.at[4]
+        if half is not None:
+            rows = pl.ds(half * (ROWS // 2), ROWS // 2)
+            src, dst = src.at[rows], dst.at[rows]
+        if k in (3, 4, 5):
+            sem = relay_recv.at[PLACE[k], half]
+        return remote(src, dst, send_sem.at[5], sem, y_device(to))
+
+    ysend[PLACE[4]] = product(4).astype(BF16)
+    for half in range(2):
+        y_copy(4, half, half).start()
+    for k in (3, 5):
+        ysend[PLACE[k]] = product(k).astype(BF16)
+    for first in range(2):
+        y_copy(3, 1 - first).start()
+        y_copy(5, first).start()
+
+    mine = tout.at[row_id]
+    take(trecv.at[pl.ds(1, NX - 1)], once_recv.at[1])
+    trecv[0] = tsend[...]
+    for h in range(HEADS):
+        parts = [trecv[k, h, :TXT_ROWS].astype(F32) for k in range(NX)]
+        levels = [to_column(trecv[k, h, TXT_ROWS:].astype(F32), TXT_ROWS) for k in range(NX)]
+        mine[:, h * HEAD_DIM:(h + 1) * HEAD_DIM] = merge(parts, levels)
+    for k in (8, 9, 7, 10, 6, 11, 5, 12, 4, 13, 3, 14, 2, 15, 1):
+        other = (row_id + k) % (2 * NZ)
+        to = device(other // 2, x, other % 2, y)
+        remote(mine, mine, send_sem.at[6], once_recv.at[5], to).start()
+
+    for way, k in enumerate((2, 6)):
+        yterm[way] = product(k)
+    for step in range(2):
+        for way, (k, relay) in enumerate(((2, 3), (6, 5))):
+            half = way if step else 1 - way
+            rows = halves[half]
+            y_copy(relay, half).wait_recv()
+            yterm[way, rows] += yrecv[PLACE[relay], rows].astype(F32)
+            if step:
+                y_copy(4, half, way).wait_recv()
+                yterm[way, rows] += yrecv[PLACE[4], rows].astype(F32)
+            ysend[PLACE[k], rows] = yterm[way, rows].astype(BF16)
+            y_copy(k, half).start()
+    for k in (1, 7):
         ysend[PLACE[k]] = product(k).astype(BF16)
         y_copy(k).start()
-
-    def x_copy(k):
-        return remote(tsend, trecv.at[k], send_sem.at[4], once_recv.at[1], x_device(k))
-
-    for h in range(HEADS):
-        part, level = finish(h, TEXT, TXT_ROWS)
-        tsend[h, :TXT_ROWS] = part.astype(BF16)
-        tsend[h, TXT_ROWS:] = to_rows(level)
-    for k in (2, 1, 3):
-        x_copy(k).start()
-    for k, relay in ((2, 3), (6, 5)):
-        yterm[...] = product(k)
-        y_copy(relay).wait_recv()
-        yterm[...] += yrecv[PLACE[relay]].astype(F32)
-        ysend[PLACE[k]] = yterm[...].astype(BF16)
-        y_copy(k).start()
     total = product(0)
 
-    mine = pl.ds(pl.multiple_of(row_id * TXT_ROWS, TXT_ROWS), TXT_ROWS)
-    take(trecv.at[pl.ds(1, NX - 1)], once_recv.at[1])
-    trecv[0] = tsend[...]
-    for h in range(HEADS):
-        parts = [trecv[k, h, :TXT_ROWS].astype(F32) for k in range(NX)]
-        levels = [to_column(trecv[k, h, TXT_ROWS:].astype(F32), TXT_ROWS) for k in range(NX)]
-        tout[mine, h * HEAD_DIM:(h + 1) * HEAD_DIM] = merge(parts, levels)
-    for k in range(1, 2 * NZ):
-        remote(tout.at[mine], tout.at[mine], send_sem.at[6], once_recv.at[5], text_device(k)).start()
-
-    take(yrecv.at[pl.ds(2, 5)], once_recv.at[4])
-    for k in (1, 2, 4, 6, 7):
+    take(yrecv.at[pl.ds(3, 4)], once_recv.at[4])
+    for k in (1, 2, 6, 7):
         total = total + yrecv[PLACE[k]].astype(F32)
     out[...] = total.astype(BF16)
 
-    rest = tout.at[pl.ds(0, (2 * NZ - 1) * TXT_ROWS)]
-    take(rest, once_recv.at[5])
+    others = tout.at[pl.ds(0, 2 * NZ - 1)]
+    take(others, once_recv.at[5])
     for index, ref in enumerate((kv.at[:, pl.ds(0, 7), 0], kv.at[:, :, 0],
                                  q.at[pl.ds(GROUP[1], 3 * ROWS)], osend,
-                                 trecv.at[pl.ds(1, NX - 1)], ysend, rest)):
+                                 trecv.at[pl.ds(1, NX - 1)], ysend, others, fsend)):
         take(ref, send_sem.at[index])
 
 
@@ -347,11 +396,11 @@
     dma = pltpu.SemaphoreType.DMA
     in_hbm = functools.partial(pltpu.with_memory_space_constraint, memory_space=pltpu.HBM)
     regular = pltpu.SemaphoreType.REGULAR
-    return pl.pallas_call(
+    video, text = pl.pallas_call(
         body,
         out_shape=(
             jax.ShapeDtypeStruct((ROWS, FEATURES), BF16),
-            jax.ShapeDtypeStruct((2 * NZ * TXT_ROWS, FEATURES), BF16),
+            jax.ShapeDtypeStruct((2 * NZ, TXT_ROWS, FEATURES), BF16),
         ),
         in_specs=[hbm] * 6 + [hbm, hbm],
         out_specs=(vmem, vmem),
@@ -366,23 +415,27 @@
             pltpu.VMEM((HEADS, NX - 1, ROWS + 16, HEAD_DIM), BF16),
             pltpu.VMEM((HEADS, TXT_ROWS + 16, HEAD_DIM), BF16),
             pltpu.VMEM((NX, HEADS, TXT_ROWS + 16, HEAD_DIM), BF16),
+            pltpu.VMEM((HEADS, TXT_ROWS + 16, HEAD_DIM), BF16),
+            pltpu.VMEM((HEADS, TXT_ROWS + 16, HEAD_DIM), BF16),
             pltpu.VMEM((ROWS, FEATURES), BF16),
             pltpu.VMEM((NY, FEATURES, FEATURES), BF16),
             pltpu.VMEM((NY - 1, ROWS, FEATURES), BF16),
             pltpu.VMEM((NY - 1, ROWS, FEATURES), BF16),
-            pltpu.VMEM((ROWS, FEATURES), F32),
+            pltpu.VMEM((2, ROWS, FEATURES), F32),
             pltpu.SMEM((TILES, TILES), jnp.int32),
-            dma((6,)),
             dma((7,)),
+            dma((8,)),
             dma((HEADS, 2, 4)),
             dma((HEADS, 5)),
             dma((HEADS, NX - 1)),
-            dma((6,)),
-            regular((3,)), regular((3,)),
+            dma((7,)),
+            dma((3, 2)),
+            regular((6,)), regular((6,)),
         ],
         compiler_params=pltpu.CompilerParams(
             collective_id=0, has_side_effects=True, vmem_limit_bytes=40 * 2**20),
     )(*map(in_hbm, (video_q, video_k, video_v, text_q, text_k, text_v, tile_mask, out_weight)))
+    return video, text.reshape(2 * NZ * TXT_ROWS, FEATURES)
 
 
 def solution(mesh):

time: 44.6 us -> 43.7 us (0.980)
  the two profiles are of different devices: /device:TPU:1 before, /device:TPU:8 now
where the time goes in v5:
time: 43.7 us; the launch traced here: 43.5 us
  Pallas kernels  41.6 us (95%)
  local copies, waits for them, and re-layouts  1.3 us (3%)
  between operations  0.64 us (1%)
    pallas_call x1, Pallas kernels, local(): pl.pallas_call(body, out_shape=(jax.ShapeDtypeStruct((ROWS, FEATURES), BF...  41.6 us
    unnamed x2, local copies, waits for them, and re-layouts  1.3 us

profile of v5, /device:TPU:8, one launch (start us, length us, event | category | flops | bytes accessed | tf_op | source)
XLA Modules:
  0.0 43.5 jit_solution(12138055665436959627)
XLA Ops:
  0.6 41.6 %shard_map.95 = (bf16[64,384]{1,0:T(8,128)(2,1)S(1)}, bf16[16,16,384]{2,1,0:T(8,128)(2,1)S(1)}) custom-call(bf16[64,384]{1,0:T(8,128)(2,1)} %vq.1, bf16[64,384]{1,0:T(8,128)(2,1)} %vk.1, bf16[64,384]{1,0:T(8,128)(2,1)} %vv.1, bf16[256,384]{1,0:T(8,128)(2,1)} %tq.1, bf16[256,384]{1,0:T(8,128)(2,1)} %tk.1, bf16[256,384]{1,0:T(8,128)(2,1)} %tv.1, ...), custom_call_target="tpu_custom_call" | custom-call | tf_op jit(solution)/shard_map/pallas_call | solution.py:399
  42.2 0.6 %copy.12 = bf16[64,384]{1,0:T(8,128)(2,1)} copy(bf16[64,384]{1,0:T(8,128)(2,1)S(1)} %get-tuple-element.8) | data formatting | bytes 98304
  42.8 0.7 %copy.13 = bf16[256,384]{1,0:T(8,128)(2,1)} copy(bf16[256,384]{1,0:T(8,128)(2,1)S(1)} %bitcast.1) | data formatting | bytes 393216

commit v6 on v5

--- a/solution.py
+++ b/solution.py
@@ -97,13 +97,12 @@
     pl.semaphore_wait(barrier, len(peers))
     for h in range(HEADS):
         for direction in range(2):
-            z_copy(h, 0, direction, 1).start()
-            z_copy(h, 1, direction, 1).start()
+            for part in range(2):
+                z_copy(h, part, direction, 1).start()
+        for part in range(2):
+            s_own(h, part).start()
     for k in (2, 1, 3):
         q_copy(k).start()
-    for h in range(HEADS):
-        for part in range(2):
-            s_own(h, part).start()
     load(mask, reach, 0)
     for h in range(HEADS):
         for part, ref in enumerate((vk, vv)):
@@ -189,8 +188,7 @@
             take(ref, z_recv.at[h, direction, d - 1])
             if d < 4:
                 z_copy(h, direction if d == 3 else None, direction, d + 1).start()
-        for place in (slot(0, d), slot(1, d)) if d < 4 else (1,):
-            s_copy(h, place, d).start()
+        s_copy(h, pl.ds(2 * d, 2) if d < 4 else 1, d).start()
 
     def from_sibling(h, s):
         places = {0: 0, 4: 1}.get(s, pl.ds(2 * s, 2))
@@ -354,7 +352,7 @@
         parts = [trecv[k, h, :TXT_ROWS].astype(F32) for k in range(NX)]
         levels = [to_column(trecv[k, h, TXT_ROWS:].astype(F32), TXT_ROWS) for k in range(NX)]
         mine[:, h * HEAD_DIM:(h + 1) * HEAD_DIM] = merge(parts, levels)
-    for k in (8, 9, 7, 10, 6, 11, 5, 12, 4, 13, 3, 14, 2, 15, 1):
+    for k in range(1, 2 * NZ):
         other = (row_id + k) % (2 * NZ)
         to = device(other // 2, x, other % 2, y)
         remote(mine, mine, send_sem.at[6], once_recv.at[5], to).start()

time: 43.7 us -> 43.7 us (level)
  no operation moved by 1% of the time
where the time goes in v6:
time: 43.7 us; the launch traced here: 43.5 us
  Pallas kernels  41.6 us (95%)
  local copies, waits for them, and re-layouts  1.3 us (3%)
  between operations  0.64 us (1%)
    pallas_call x1, Pallas kernels, local(): pl.pallas_call(body, out_shape=(jax.ShapeDtypeStruct((ROWS, FEATURES), BF...  41.6 us
    unnamed x2, local copies, waits for them, and re-layouts  1.3 us

profile of v6, /device:TPU:8, one launch (start us, length us, event | category | flops | bytes accessed | tf_op | source)
XLA Modules:
  0.0 43.5 jit_solution(9588144471430253412)
XLA Ops:
  0.6 41.6 %shard_map.95 = (bf16[64,384]{1,0:T(8,128)(2,1)S(1)}, bf16[16,16,384]{2,1,0:T(8,128)(2,1)S(1)}) custom-call(bf16[64,384]{1,0:T(8,128)(2,1)} %vq.1, bf16[64,384]{1,0:T(8,128)(2,1)} %vk.1, bf16[64,384]{1,0:T(8,128)(2,1)} %vv.1, bf16[256,384]{1,0:T(8,128)(2,1)} %tq.1, bf16[256,384]{1,0:T(8,128)(2,1)} %tk.1, bf16[256,384]{1,0:T(8,128)(2,1)} %tv.1, ...), custom_call_target="tpu_custom_call" | custom-call | tf_op jit(solution)/shard_map/pallas_call | solution.py:397
  42.2 0.6 %copy.12 = bf16[64,384]{1,0:T(8,128)(2,1)} copy(bf16[64,384]{1,0:T(8,128)(2,1)S(1)} %get-tuple-element.8) | data formatting | bytes 98304
  42.8 0.7 %copy.13 = bf16[256,384]{1,0:T(8,128)(2,1)} copy(bf16[256,384]{1,0:T(8,128)(2,1)S(1)} %bitcast.1) | data formatting | bytes 393216

commit v7 on v5

--- a/solution.py
+++ b/solution.py
@@ -177,6 +177,8 @@
         summed = jnp.dot(weights, values, preferred_element_type=F32)
         if s:
             summed = summed + acc[h, :used] * jnp.exp2(before - high)
+        if s == 4:
+            return summed[:, :HEAD_DIM] / summed[:, HEAD_DIM:]
         acc[h, :used] = summed
         top[h, :used] = jnp.broadcast_to(high, (used, HEAD_DIM))
 
@@ -317,11 +319,7 @@
     for h in range(HEADS):
         from_sibling(h, 4)
     for h in range(HEADS):
-        absorb(h, 4)
-    own = slice(GROUP[0], GROUP[0] + ROWS)
-    for h in range(HEADS):
-        attn[:, h * HEAD_DIM:(h + 1) * HEAD_DIM] = (
-            acc[h, own, :HEAD_DIM] / acc[h, own, HEAD_DIM:]).astype(BF16)
+        attn[:, h * HEAD_DIM:(h + 1) * HEAD_DIM] = absorb(h, 4).astype(BF16)
 
     def product(k):
         return jnp.dot(attn[...], wbuf[k], preferred_element_type=F32)

time: 43.7 us -> 43.7 us (level)
  no operation moved by 1% of the time
where the time goes in v7:
time: 43.7 us; the launch traced here: 43.5 us
  Pallas kernels  41.6 us (95%)
  local copies, waits for them, and re-layouts  1.3 us (3%)
  between operations  0.64 us (1%)
    pallas_call x1, Pallas kernels, local(): pl.pallas_call(body, out_shape=(jax.ShapeDtypeStruct((ROWS, FEATURES), BF...  41.6 us
    unnamed x2, local copies, waits for them, and re-layouts  1.3 us

profile of v7, /device:TPU:8, one launch (start us, length us, event | category | flops | bytes accessed | tf_op | source)
XLA Modules:
  0.0 43.5 jit_solution(12138055665436959627)
XLA Ops:
  0.6 41.6 %shard_map.95 = (bf16[64,384]{1,0:T(8,128)(2,1)S(1)}, bf16[16,16,384]{2,1,0:T(8,128)(2,1)S(1)}) custom-call(bf16[64,384]{1,0:T(8,128)(2,1)} %vq.1, bf16[64,384]{1,0:T(8,128)(2,1)} %vk.1, bf16[64,384]{1,0:T(8,128)(2,1)} %vv.1, bf16[256,384]{1,0:T(8,128)(2,1)} %tq.1, bf16[256,384]{1,0:T(8,128)(2,1)} %tk.1, bf16[256,384]{1,0:T(8,128)(2,1)} %tv.1, ...), custom_call_target="tpu_custom_call" | custom-call | tf_op jit(solution)/shard_map/pallas_call | solution.py:397
  42.2 0.6 %copy.12 = bf16[64,384]{1,0:T(8,128)(2,1)} copy(bf16[64,384]{1,0:T(8,128)(2,1)S(1)} %get-tuple-element.8) | data formatting | bytes 98304
  42.8 0.7 %copy.13 = bf16[256,384]{1,0:T(8,128)(2,1)} copy(bf16[256,384]{1,0:T(8,128)(2,1)S(1)} %bitcast.1) | data formatting | bytes 393216
